TPU v7x, 256 devices: a whole 4x4x8 slice. The times are simulated.
256 devices in a mesh: ctx: 32 (over x, z), tp: 8 (over y, core).
Axes of the slice: x: 4, y: 4, z: 8, core: 2. Of those that a mesh axis runs over, the one named last changes fastest.
Arguments:
- first_input: bfloat16 [8192, 8192], P('ctx', 'tp'), may hold values from -6 to 6
- second_input: bfloat16 [8192, 8192], P('ctx', 'tp'), may hold values from -6 to 6
- value_input: bfloat16 [8192, 8192], P('ctx', 'tp'), may hold values from -6 to 6
- filter_taps: bfloat16 [8192, 8192], P('ctx', 'tp'), may hold values from -1.5 to 1.5
- skip_gain: float32 [8192], P('tp'), may hold values from -1 to 1
- out_weight: bfloat16 [8192, 4096], P('tp'), may hold values from -0.0625 to 0.0625
- queries: bfloat16 [8192, 4096], P('ctx', 'tp'), may hold values from -6 to 6
- keys: bfloat16 [8192, 4096], P('ctx', 'tp'), may hold values from -6 to 6
Outputs:
- mixed: bfloat16 [8192, 4096], P('ctx', 'tp')
- attended: bfloat16 [8192, 4096], P('ctx', 'tp')
All inputs are finite; a program needn't handle non-finite values.
Results may differ from a plain program's by a relative error of at most 0.02.
Values may be sent and summed in bfloat16 or wider, within the bound.
A program may use at most 256 MiB of HBM per device.

v0:
```python
import functools
import math

import jax
import jax.numpy as jnp
import numpy as np
from jax import lax
from jax.experimental import pallas as pl
from jax.experimental.pallas import tpu as pltpu
from jax.sharding import PartitionSpec as P

HS = 128
MESH = pl.DeviceIdType.MESH
BF = jnp.bfloat16
F32 = jnp.float32
CTX = 32
ROWS = 256
GROUP = 16
TOTAL = CTX * ROWS


def nt(a, b):
    return lax.dot_general(a, b, (((1,), (1,)), ((), ())), preferred_element_type=F32)


def nn(a, b):
    return jnp.dot(a, b, preferred_element_type=F32)


def tables():
    r = np.arange(CTX, dtype=np.float64)
    q = np.arange(CTX, dtype=np.float64)
    a = np.arange(ROWS, dtype=np.float64)
    rows = np.exp(-2j * np.pi * np.outer(q + 0.25, r) / CTX)
    turn = np.exp(-2j * np.pi * np.outer(q + 0.25, a) / TOTAL)
    cols = np.exp(-2j * np.pi * np.outer(a, a) / ROWS)
    eye = np.eye(GROUP)
    spread = lambda m: np.einsum("qr,cd->cqrd", m, eye).reshape(GROUP * CTX, CTX * GROUP)
    first = np.concatenate([spread(rows.real), spread(rows.imag)], axis=0)
    back = np.conj(rows).T
    gather = lambda m: np.einsum("rq,cd->rcdq", m, eye).reshape(CTX * GROUP, GROUP * CTX)
    last = np.concatenate([gather(back.real), -gather(back.imag)], axis=1)
    mix = np.block([[cols.real, cols.imag], [-cols.imag, cols.real]])
    unmix = np.block([[cols.real, -cols.imag], [cols.imag, cols.real]]) / TOTAL
    cast = lambda m: np.asarray(m, np.float32).astype(jnp.bfloat16)
    return (cast(first), cast(mix), cast(unmix), cast(last),
            np.asarray(turn.real, np.float32), np.asarray(turn.imag, np.float32))


def spectrum(x, first, mix, turn_re, turn_im):
    half = GROUP * CTX
    a = nn(first, x)
    a_re = a[:half].reshape(GROUP, CTX, ROWS)
    a_im = a[half:].reshape(GROUP, CTX, ROWS)
    z_re = (a_re * turn_re - a_im * turn_im).reshape(half, ROWS).astype(BF)
    z_im = (a_re * turn_im + a_im * turn_re).reshape(half, ROWS).astype(BF)
    return nn(jnp.concatenate([z_re, z_im], axis=1), mix)


def filter_kernel(
    first_ref, value_ref, taps_ref, second_ref, skip_ref, eye_ref, first_t, mix_t, unmix_t, last_t,
    turn_re, turn_im, gated_ref, product, send, recv, out_send, out_recv,
    send_sem, recv_sem, back_send_sem, back_recv_sem,
):
    me = lax.axis_index("ctx")
    half = GROUP * CTX
    barrier = pltpu.get_barrier_semaphore()

    def greet(k, carry):
        pl.semaphore_signal(
            barrier, inc=1, device_id={"ctx": lax.rem(me + k, CTX)}, device_id_type=MESH
        )
        return carry

    lax.fori_loop(1, CTX, greet, 0)
    eye = eye_ref[...]
    for cb in range(4):
        cols = slice(cb * 256, (cb + 1) * 256)
        prod = (first_ref[:, cols].astype(F32) * value_ref[:, cols].astype(F32)).astype(BF)
        product[:, cols] = prod
        for kind, block in ((0, prod), (1, taps_ref[:, cols])):
            turned = nt(eye, block).astype(BF)
            for dl in range(8):
                for h in range(2):
                    at = dl * 32 + h * GROUP
                    send[h, cb * 8 + dl, kind] = turned[at:at + GROUP]
    pl.semaphore_wait(barrier, CTX - 1)

    for h in range(2):
        def post(k, carry, h=h):
            to = lax.rem(me + k, CTX)
            pltpu.make_async_remote_copy(
                src_ref=send.at[h, to], dst_ref=recv.at[h, me],
                send_sem=send_sem.at[h], recv_sem=recv_sem.at[h],
                device_id={"ctx": to}, device_id_type=MESH,
            ).start()
            return carry

        pltpu.make_async_copy(send.at[h, me], recv.at[h, me], recv_sem.at[h]).start()
        lax.fori_loop(1, CTX, post, 0)

    for h in range(2):
        pltpu.make_async_copy(recv.at[h], recv.at[h], recv_sem.at[h]).wait()
        tr, ti = turn_re[...], turn_im[...]
        x = recv[h, :, 0].reshape(half, ROWS)
        w = recv[h, :, 1].reshape(half, ROWS)
        d = spectrum(x, first_t[...], mix_t[...], tr, ti)
        e = spectrum(w, first_t[...], mix_t[...], tr, ti)
        d_re, d_im, e_re, e_im = d[:, :ROWS], d[:, ROWS:], e[:, :ROWS], e[:, ROWS:]
        y_re = (d_re * e_re - d_im * e_im).astype(BF)
        y_im = (d_re * e_im + d_im * e_re).astype(BF)
        b = nn(jnp.concatenate([y_re, y_im], axis=1), unmix_t[...])
        b_re = b[:, :ROWS].reshape(GROUP, CTX, ROWS)
        b_im = b[:, ROWS:].reshape(GROUP, CTX, ROWS)
        c_re = (b_re * tr + b_im * ti).reshape(half, ROWS).astype(BF)
        c_im = (b_im * tr - b_re * ti).reshape(half, ROWS).astype(BF)
        y = nn(last_t[...], jnp.concatenate([c_re, c_im], axis=0))
        out_send[h] = y.astype(BF).reshape(CTX, GROUP, ROWS)

        def reply(k, carry, h=h):
            to = lax.rem(me + k, CTX)
            pltpu.make_async_remote_copy(
                src_ref=out_send.at[h, to], dst_ref=out_recv.at[h, me],
                send_sem=back_send_sem.at[h], recv_sem=back_recv_sem.at[h],
                device_id={"ctx": to}, device_id_type=MESH,
            ).start()
            return carry

        pltpu.make_async_copy(out_send.at[h, me], out_recv.at[h, me], back_recv_sem.at[h]).start()
        lax.fori_loop(1, CTX, reply, 0)

    for h in range(2):
        sent = send.at[h, pl.ds(0, CTX - 1)]
        pltpu.make_async_copy(sent, sent, send_sem.at[h]).wait()
    for h in range(2):
        pltpu.make_async_copy(out_recv.at[h], out_recv.at[h], back_recv_sem.at[h]).wait()
        sent = out_send.at[h, pl.ds(0, CTX - 1)]
        pltpu.make_async_copy(sent, sent, back_send_sem.at[h]).wait()
    for cb in range(4):
        cols = slice(cb * 256, (cb + 1) * 256)
        parts = [out_recv[h, cb * 8 + dl] for dl in range(8) for h in range(2)]
        filtered = nt(eye, jnp.concatenate(parts, axis=0)).astype(BF).astype(F32)
        prod = product[:, cols].astype(F32)
        gated_ref[:, cols] = (
            second_ref[:, cols].astype(F32) * (filtered + skip_ref[:, cols] * prod)
        ).astype(BF)


def vmem(count):
    return [pl.BlockSpec(memory_space=pltpu.VMEM)] * count


def filtered_and_gated(first_input, value_input, filter_taps, second_input, skip_gain):
    first, mix, unmix, last, turn_re, turn_im = (jnp.asarray(t) for t in tables())
    eye = jnp.eye(ROWS, dtype=BF)
    return pl.pallas_call(
        filter_kernel,
        out_shape=jax.ShapeDtypeStruct((ROWS, 1024), BF),
        in_specs=vmem(12),
        out_specs=pl.BlockSpec(memory_space=pltpu.VMEM),
        scratch_shapes=[
            pltpu.VMEM((ROWS, 1024), BF),
            pltpu.VMEM((2, CTX, 2, GROUP, ROWS), BF),
            pltpu.VMEM((2, CTX, 2, GROUP, ROWS), BF),
            pltpu.VMEM((2, CTX, GROUP, ROWS), BF),
            pltpu.VMEM((2, CTX, GROUP, ROWS), BF),
            pltpu.SemaphoreType.DMA((2,)),
            pltpu.SemaphoreType.DMA((2,)),
            pltpu.SemaphoreType.DMA((2,)),
            pltpu.SemaphoreType.DMA((2,)),
        ],
        compiler_params=pltpu.CompilerParams(
            collective_id=0, has_side_effects=True, vmem_limit_bytes=40 * 1024 * 1024
        ),
        name="filter_and_gate",
    )(first_input, value_input, filter_taps, second_input, skip_gain.reshape(1, 1024), eye,
      first, mix, unmix, last, turn_re, turn_im)


BIG_NEGATIVE = -1e30


def fold_block(state, query_heads, query_pos, key_heads, value_heads, key_pos, score_scale):
    top_score, weight_sum, weighted = state
    scores = (
        jnp.einsum("qhd,khd->qhk", query_heads, key_heads, preferred_element_type=jnp.float32)
        * score_scale
    )
    allowed = (key_pos[None, :] <= query_pos[:, None])[:, None, :]
    scores = jnp.where(allowed, scores, BIG_NEGATIVE)
    new_top = jnp.maximum(top_score, jnp.max(scores, axis=2))
    weights = jnp.where(allowed, jnp.exp(scores - new_top[:, :, None]), 0.0)
    shrink = jnp.exp(top_score - new_top)
    weight_sum = weight_sum * shrink + jnp.sum(weights, axis=2)
    weighted = weighted * shrink[:, :, None] + jnp.einsum(
        "qhk,khd->qhd",
        weights.astype(jnp.bfloat16),
        value_heads,
        preferred_element_type=jnp.float32,
    )
    return (new_top, weight_sum, weighted)


def fold_keys(state, query_heads, query_pos, key_heads, value_heads, key_pos, score_scale):
    key_rows = key_heads.shape[0]
    step_rows = 1024

    def scan_step(carry, step_index):
        first_row = step_index * step_rows
        key_part = lax.dynamic_slice_in_dim(key_heads, first_row, step_rows, 0)
        value_part = lax.dynamic_slice_in_dim(value_heads, first_row, step_rows, 0)
        pos_part = lax.dynamic_slice_in_dim(key_pos, first_row, step_rows, 0)
        return (
            fold_block(carry, query_heads, query_pos, key_part, value_part, pos_part, score_scale),
            None,
        )

    state, leftover = lax.scan(scan_step, state, jnp.arange(key_rows // step_rows, dtype=jnp.int32))
    return state


def per_device(
    first_input, second_input, value_input, filter_taps, skip_gain, out_weight, queries, keys
):
    tok_rows = first_input.shape[0]
    gated = filtered_and_gated(
        first_input, value_input, filter_taps, second_input, skip_gain
    )
    partial_sums = jnp.dot(gated, out_weight, preferred_element_type=jnp.float32)
    mixed = lax.psum_scatter(
        partial_sums.astype(jnp.bfloat16), "tp", scatter_dimension=1, tiled=True
    )
    head_count = queries.shape[1] // HS
    score_scale = 1.0 / math.sqrt(HS)
    ctx_rank = lax.axis_index("ctx")
    query_pos = ctx_rank * tok_rows + jnp.arange(tok_rows, dtype=jnp.int32)
    row_spans = ((0, tok_rows),)
    query_heads = queries.reshape(tok_rows, head_count, HS)
    initial = (
        jnp.full((tok_rows, head_count), BIG_NEGATIVE, jnp.float32),
        jnp.zeros((tok_rows, head_count), jnp.float32),
        jnp.zeros((tok_rows, head_count, HS), jnp.float32),
    )
    key_piece = lax.all_gather(keys, "ctx", axis=0, tiled=True)
    value_piece = lax.all_gather(mixed, "ctx", axis=0, tiled=True)
    piece_rows = key_piece.shape[0]
    key_heads = key_piece.reshape(piece_rows, head_count, HS)
    value_heads = value_piece.reshape(piece_rows, head_count, HS)
    key_pos = jnp.arange(piece_rows, dtype=jnp.int32)
    span_start, span_stop = row_spans[0]
    sub_state = (initial[0], initial[1], initial[2])

    def visit(inner_state, span_start=span_start, span_stop=span_stop):
        return fold_keys(
            inner_state, query_heads, query_pos, key_heads, value_heads, key_pos, score_scale
        )

    def unchanged(inner_state):
        return inner_state

    sub_state = lax.cond(jnp.int32(0) <= query_pos[span_stop - 1], visit, unchanged, sub_state)
    span_states = [sub_state]
    top_score, weight_sum, weighted = tuple(
        (
            jnp.concatenate([group_state[member_index] for group_state in span_states], axis=0)
            for member_index in range(3)
        )
    )
    outcome = (
        (weighted / weight_sum[:, :, None]).reshape(tok_rows, head_count * HS).astype(jnp.bfloat16)
    )
    return (mixed, outcome)


def solution(mesh):
    return jax.shard_map(
        per_device,
        mesh=mesh,
        in_specs=(
            P("ctx", "tp"),
            P("ctx", "tp"),
            P("ctx", "tp"),
            P("ctx", "tp"),
            P("tp"),
            P("tp", None),
            P("ctx", "tp"),
            P("ctx", "tp"),
        ),
        out_specs=(P("ctx", "tp"), P("ctx", "tp")),
        check_vma=False,
    )
```

profile of v0, /device:TPU:6, one launch (start us, length us, event | category | flops | bytes accessed | tf_op | source)
XLA Modules:
  0.0 372.0 jit_solution(17774819428796168170)
XLA Ops:
  19.0 46.8 %filter_and_gate.1 = bf16[256,1024]{1,0:T(8,128)(2,1)S(1)} custom-call(bf16[256,1024]{1,0:T(8,128)(2,1)S(1)} %copy-done.2, bf16[256,1024]{1,0:T(8,128)(2,1)S(1)} %copy-done.3, bf16[256,1024]{1,0:T(8,128)(2,1)S(1)} %copy-done.4, bf16[256,1024]{1,0:T(8,128)(2,1)S(1)} %copy-done.5, f32[1,1024]{1,0:T(1,128)S(1)} %bitcast.41, ...), custom_call_target="tpu_custom_call" | custom-call | tf_op jit(solution)/shard_map/filter_and_gate/pallas_call | solution.py:156
  65.8 7.2 %convolution_convert_fusion = bf16[256,4096]{1,0:T(8,128)(2,1)} fusion(bf16[256,1024]{1,0:T(8,128)(2,1)S(1)} %filter_and_gate.1, bf16[1024,4096]{1,0:T(8,128)(2,1)} %param.23), kind=kOutput, calls=%fused_computation.23 | convolution fusion | flops 2148532224 | bytes 11010048 | tf_op jit(solution)/shard_map/dot_general | solution.py:229
  74.0 33.8 %reduce-scatter.2.cloned.1.call-done = bf16[256,512]{1,0:T(8,128)(2,1)} async-done(((bf16[256,4096]{1,0:T(8,128)(2,1)}), bf16[256,512]{1,0:T(8,128)(2,1)}) %reduce-scatter.2.cloned.1.call-update) | async-done | bytes 262160 | tf_op jit(solution)/shard_map/reduce_scatter | solution.py:230
  108.9 67.6 %all-gather.3.cloned.1.call-done = bf16[8192,512]{0,1:T(8,128)(2,1)} async-done(((bf16[256,512]{0,1:T(8,128)(2,1)}), bf16[8192,512]{0,1:T(8,128)(2,1)}) %all-gather.3.cloned.1.call-update) | async-done | bytes 8388624 | tf_op jit(solution)/shard_map/all_gather | solution.py:244
  176.5 99.1 %all-gather.5.cloned.1.call-done = bf16[8192,512]{1,0:T(8,128)(2,1)} async-done(((bf16[256,512]{1,0:T(8,128)(2,1)}), bf16[8192,512]{1,0:T(8,128)(2,1)}) %all-gather.5.cloned.1.call-update) | async-done | bytes 8388624 | tf_op jit(solution)/shard_map/all_gather | solution.py:245
  275.6 87.0 %conditional.1 = (f32[256,4]{0,1:T(4,128)}, f32[256,4,128]{0,2,1:T(8,128)}) conditional(s32[]{:T(128)} %bitcast.4, () %tuple.20, (bf16[8192,512]{0,1:T(8,128)(2,1)}, bf16[8192,512]{1,0:T(8,128)(2,1)}, bf16[256,512]{1,0:T(8,128)(2,1)S(1)}, s32[8192]{0:T(1024)S(1)}, s32[256]{0:T(256)S(1)}) %tuple.57), branch_computations={%region_1.0_spmd, %region_2.7_spmd} | conditional | flops 551162880 | bytes 34944392 | solution.py:261
  275.9 12.0 %copy.24 = bf16[8192,512]{0,1:T(8,128)(2,1)} copy(bf16[8192,512]{1,0:T(8,128)(2,1)} %get-tuple-element.128) | data formatting | bytes 16777216 | tf_op jit(solution)/shard_map
  288.0 74.6 %while.14 = (s32[]{:T(128)}, f32[256,4]{0,1:T(4,128)S(1)}, f32[256,4]{0,1:T(4,128)}, f32[256,4,128]{0,2,1:T(8,128)}, s32[8]{0:T(128)S(1)}, /*index=5*/s32[8192]{...) while((s32[]{:T(128)}, f32[256,4]{0,1:T(4,128)S(1)}, ...), condition=%wide.region_6.6_spmd.clone, body=%wide.region_3.5_spmd.clone.sunk | while | flops 551162880 | bytes 17118432 | solution.py:218
  289.4 2.2 fusion.35
  293.3 3.3 fusion.38
  298.1 2.2 fusion.35
  302.6 3.4 fusion.38
  307.5 2.2 fusion.35
  312.0 3.4 fusion.38
  316.9 2.2 fusion.35
  321.5 3.4 fusion.38
  326.4 2.2 fusion.35
  330.9 3.4 fusion.38
  335.8 2.2 fusion.35
  340.3 3.4 fusion.38
  345.2 2.2 fusion.35
  349.8 3.4 fusion.38
  354.6 2.2 fusion.35
  359.2 3.4 fusion.38
  (101 shorter events, 39.3 us)
Async XLA Ops:
  8.0 99.8 %reduce-scatter.2.cloned.1.call-start = ((), (), s32[]{:S(2)}) async-start(), calls=%async_computation.1 | async-start | bytes 2359296 | tf_op jit(solution)/shard_map/reduce_scatter | solution.py:230
  8.1 1.2 copy-start
  9.3 1.2 copy-start.1
  10.5 1.0 copy-start.2
  11.6 1.0 copy-start.3
  12.6 1.0 copy-start.4
  13.6 1.0 copy-start.5
  14.7 1.0 copy-start.6
  15.7 1.0 copy-start.7
  16.8 0.8 copy-start.8
  17.5 0.8 copy-start.9
  18.3 0.7 copy-start.10
  65.8 7.3 %copy-start.11 = (bf16[256,512]{1,0:T(8,128)(2,1)S(1)}, bf16[256,512]{1,0:T(8,128)(2,1)}, u32[]{:S(2)}) copy-start(bf16[256,512]{1,0:T(8,128)(2,1)} %param.25) | copy-start | bytes 786436
  65.8 209.8 %copy-start.12 = (bf16[256,512]{1,0:T(8,128)(2,1)S(1)}, bf16[256,512]{1,0:T(8,128)(2,1)}, u32[]{:S(2)}) copy-start(bf16[256,512]{1,0:T(8,128)(2,1)} %param.24) | copy-start | bytes 786436
  73.0 103.5 %all-gather.3.cloned.1.call-start = ((), (), s32[]{:S(2)}) async-start(), calls=%async_computation.2 | async-start | bytes 8650752 | tf_op jit(solution)/shard_map/all_gather | solution.py:244
  73.9 201.6 %all-gather.5.cloned.1.call-start = ((), (), s32[]{:S(2)}) async-start(), calls=%async_computation.3 | async-start | bytes 8650752 | tf_op jit(solution)/shard_map/all_gather | solution.py:245
Sparse Core Ops, SparseCore 0:
  73.1 34.5 reduce-scatter.1
Sparse Core Ops, SparseCore 1:
  76.5 99.9 all-gather.2
  179.5 96.0 all-gather.4
where the time goes:
time: 376 us; the launch traced here: 372 us
  waiting for transfers between devices  200 us (53%)
  matrix products  51.9 us (14%)
  Pallas kernels  46.8 us (12%)
  local copies, waits for them, and re-layouts  30.3 us (8%)
  other arithmetic  20.8 us (6%)
  between operations  16.1 us (4%)
  loops' own time  5.36 us (1%)
    all_gather x1, waiting for transfers between devices, per_device(): value_piece = lax.all_gather(mixed, 'ctx', axis=0, tiled=True)  99.1 us
    all_gather x1, waiting for transfers between devices, per_device(): key_piece = lax.all_gather(keys, 'ctx', axis=0, tiled=True)  67.6 us
    pallas_call x1, Pallas kernels, filtered_and_gated(): pl.pallas_call(filter_kernel, out_shape=jax.ShapeDtypeStruct((ROWS, 1024)...  46.8 us
    reduce_scatter x1, waiting for transfers between devices, per_device(): lax.psum_scatter(partial_sums.astype(jnp.bfloat16), 'tp', scatter_dimensi...  33.8 us
    dot_general x8, matrix products, fold_block(): jnp.einsum('qhk,khd->qhd', weights.astype(jnp.bfloat16), value_heads, pre...  27.2 us
    dot_general x8, matrix products, fold_block(): jnp.einsum('qhd,khd->qhk', query_heads, key_heads, preferred_element_type...  17.6 us
    another operation x2, local copies, waits for them, and re-layouts  12.2 us
    unnamed x27, local copies, waits for them, and re-layouts  11.7 us
  transfers between devices with their start and end apart: 3, of which 3 were waited for; matrix products, arithmetic and copies ran while one was open for 0% of the time, Pallas kernels for 0%

commit v1 on v0

--- a/solution.py
+++ b/solution.py
@@ -177,99 +177,339 @@
       first, mix, unmix, last, turn_re, turn_im)
 
 
-BIG_NEGATIVE = -1e30
-
-
-def fold_block(state, query_heads, query_pos, key_heads, value_heads, key_pos, score_scale):
-    top_score, weight_sum, weighted = state
-    scores = (
-        jnp.einsum("qhd,khd->qhk", query_heads, key_heads, preferred_element_type=jnp.float32)
-        * score_scale
-    )
-    allowed = (key_pos[None, :] <= query_pos[:, None])[:, None, :]
-    scores = jnp.where(allowed, scores, BIG_NEGATIVE)
-    new_top = jnp.maximum(top_score, jnp.max(scores, axis=2))
-    weights = jnp.where(allowed, jnp.exp(scores - new_top[:, :, None]), 0.0)
-    shrink = jnp.exp(top_score - new_top)
-    weight_sum = weight_sum * shrink + jnp.sum(weights, axis=2)
-    weighted = weighted * shrink[:, :, None] + jnp.einsum(
-        "qhk,khd->qhd",
-        weights.astype(jnp.bfloat16),
-        value_heads,
-        preferred_element_type=jnp.float32,
-    )
-    return (new_top, weight_sum, weighted)
-
-
-def fold_keys(state, query_heads, query_pos, key_heads, value_heads, key_pos, score_scale):
-    key_rows = key_heads.shape[0]
-    step_rows = 1024
-
-    def scan_step(carry, step_index):
-        first_row = step_index * step_rows
-        key_part = lax.dynamic_slice_in_dim(key_heads, first_row, step_rows, 0)
-        value_part = lax.dynamic_slice_in_dim(value_heads, first_row, step_rows, 0)
-        pos_part = lax.dynamic_slice_in_dim(key_pos, first_row, step_rows, 0)
-        return (
-            fold_block(carry, query_heads, query_pos, key_part, value_part, pos_part, score_scale),
-            None,
+XS, ZS, YS = 4, 8, 4
+HEAD = 512
+KEYS = 512
+NEG = -1e30
+
+
+class Spread:
+    def __init__(self, place, buf, z_send, own, left, right, far, sib, sent):
+        self.x, self.z, self.y, self.c = place
+        self.buf, self.z_send, self.own, self.left, self.right, self.far, self.sib, self.sent = (
+            buf, z_send, own, left, right, far, sib, sent
         )
-
-    state, leftover = lax.scan(scan_step, state, jnp.arange(key_rows // step_rows, dtype=jnp.int32))
-    return state
+        self.xl, self.xr, self.x2 = (lax.rem(self.x + k, XS) for k in (3, 1, 2))
+
+    def device(self, x, z, c):
+        return {"ctx": x * ZS + z, "tp": self.y * 2 + c}
+
+    def scatter(self, source, start):
+        x, z, c = self.x, self.z, self.c
+        core, i = lax.rem(z, 2), lax.div(z, 2)
+        for j in range(4):
+            to = 4 * c + j
+            alone = (to == z) & (core == c)
+            part = source.at[:, pl.ds(j * HS, HS)]
+            slot = self.buf.at[x, z]
+            local = pltpu.make_async_copy(part, slot, self.own.at[i])
+            away = pltpu.make_async_remote_copy(
+                src_ref=part, dst_ref=slot, send_sem=self.z_send.at[j], recv_sem=self.own.at[i],
+                device_id=self.device(x, to, core), device_id_type=MESH,
+            )
+            if start:
+                pl.when(alone)(local.start)
+                pl.when(jnp.logical_not(alone))(away.start)
+            else:
+                pl.when(jnp.logical_not(alone))(away.wait_send)
+
+    def push(self, block, i, x, c, sem):
+        pltpu.make_async_remote_copy(
+            src_ref=block, dst_ref=block, send_sem=self.sent.at[i], recv_sem=sem,
+            device_id=self.device(x, self.z, c), device_id_type=MESH,
+        ).start()
+
+    def arrived(self, block, sem):
+        pltpu.make_async_copy(block, block, sem).wait()
+
+    def step_own(self, i):
+        block = self.buf.at[self.x, 2 * i + self.c]
+        self.arrived(block, self.own.at[i])
+        self.push(block, i, self.xr, self.c, self.left.at[i])
+        self.push(block, i, self.xl, self.c, self.right.at[i])
+        self.push(block, i, self.x, 1 - self.c, self.sib.at[i])
+
+    def step_near(self, i):
+        zi = 2 * i + self.c
+        block = self.buf.at[self.xl, zi]
+        self.arrived(block, self.left.at[i])
+        half = self.buf.at[self.xl, zi, pl.ds(0, 128)]
+        self.push(half, i, self.xr, self.c, self.far.at[0, i])
+        self.push(block, i, self.x, 1 - self.c, self.sib.at[i])
+        block = self.buf.at[self.xr, zi]
+        self.arrived(block, self.right.at[i])
+        half = self.buf.at[self.xr, zi, pl.ds(128, 128)]
+        self.push(half, i, self.xl, self.c, self.far.at[1, i])
+        self.push(block, i, self.x, 1 - self.c, self.sib.at[i])
+
+    def step_far(self, i):
+        for h in range(2):
+            half = self.buf.at[self.x2, 2 * i + self.c, pl.ds(h * 128, 128)]
+            self.arrived(half, self.far.at[h, i])
+            self.push(half, i, self.x, 1 - self.c, self.sib.at[i])
+
+    def finish(self, i):
+        blocks = self.buf.at[:, 2 * i + 1 - self.c]
+        self.arrived(blocks, self.sib.at[i])
+        some = self.buf.at[0, pl.ds(0, 7)]
+        self.arrived(some, self.sent.at[i])
+
+
+def attend_kernel(
+    gated_ref, weight_ref, queries_ref, keys_ref, mixed_ref, attended_ref,
+    weights, own_part, sib_send, sib_recv, y_send, y_recv, near_send, near_recv, mine,
+    k_buf, v_buf, q_buf, scores, rounded, totals, o_send, o_recv,
+    w_sem, sib_send_sem, sib_recv_sem, y_send_sem, y_recv_sem, near_send_sem, near_recv_sem,
+    q_send_sem, q_recv_sem, o_send_sem, o_recv_sem,
+    kz, k_own, k_left, k_right, k_far, k_sib, k_sent,
+    vz, v_own, v_left, v_right, v_far, v_sib, v_sent,
+):
+    ctx, tp = lax.axis_index("ctx"), lax.axis_index("tp")
+    x, z = lax.div(ctx, ZS), lax.rem(ctx, ZS)
+    y, c = lax.div(tp, 2), lax.rem(tp, 2)
+    place = (x, z, y, c)
+    keys_of = Spread(place, k_buf, kz, k_own, k_left, k_right, k_far, k_sib, k_sent)
+    values_of = Spread(place, v_buf, vz, v_own, v_left, v_right, v_far, v_sib, v_sent)
+    barrier = pltpu.get_barrier_semaphore()
+
+    def greet(to_ctx, to_tp):
+        pl.semaphore_signal(
+            barrier, inc=1, device_id={"ctx": to_ctx, "tp": to_tp}, device_id_type=MESH
+        )
+
+    for k in range(1, ZS):
+        to = x * ZS + lax.rem(z + k, ZS)
+        greet(to, tp)
+        greet(to, y * 2 + 1 - c)
+    greet(ctx, y * 2 + 1 - c)
+    for k in (1, 3):
+        greet(lax.rem(x + k, XS) * ZS + z, tp)
+        greet(ctx, lax.rem(y + k, YS) * 2 + c)
+
+    order = [(other, lax.rem(y + k, YS)) for other in (1, 0) for k in (2, 1, 3, 0)]
+    loads = []
+    for k, (other, to_y) in enumerate(order):
+        col = to_y * 2 + (1 - c if other else c)
+        loads.append(pltpu.make_async_copy(
+            weight_ref.at[:, pl.ds(pl.multiple_of(col * HEAD, HEAD), HEAD)], weights.at[k], w_sem.at[k]
+        ))
+        loads[-1].start()
+    pl.semaphore_wait(barrier, 2 * (ZS - 1) + 1 + 4)
+
+    keys_of.scatter(keys_ref, True)
+    q_core = lax.rem(lax.div(z + 1, 2), 2)
+
+    def query_copies(j):
+        to = 4 * c + j
+        alone = (to == z) & (q_core == c)
+        part = queries_ref.at[:, pl.ds(j * HS, HS)]
+        slot = q_buf.at[lax.div(z, 2)]
+        sem = q_recv_sem.at[lax.div(z, 2)]
+        return alone, pltpu.make_async_copy(part, slot, sem), pltpu.make_async_remote_copy(
+            src_ref=part, dst_ref=slot, send_sem=q_send_sem.at[j], recv_sem=sem,
+            device_id={"ctx": x * ZS + to, "tp": y * 2 + q_core}, device_id_type=MESH,
+        )
+
+    for j in range(4):
+        alone, local, away = query_copies(j)
+        pl.when(alone)(local.start)
+        pl.when(jnp.logical_not(alone))(away.start)
+
+    gated = gated_ref[...]
+    swaps = []
+    for k in range(4):
+        loads[k].wait()
+        sib_send[k] = nn(gated, weights[k]).astype(BF)
+        swaps.append(pltpu.make_async_remote_copy(
+            src_ref=sib_send.at[k], dst_ref=sib_recv.at[k],
+            send_sem=sib_send_sem.at[k], recv_sem=sib_recv_sem.at[k],
+            device_id={"tp": y * 2 + 1 - c}, device_id_type=MESH,
+        ))
+        swaps[-1].start()
+    for i in range(4):
+        keys_of.step_own(i)
+    for k in range(4):
+        loads[4 + k].wait()
+        own_part[k] = nn(gated, weights[4 + k])
+    for i in range(4):
+        keys_of.step_near(i)
+
+    def chip_sum(k):
+        swaps[k].wait_recv()
+        return own_part[k] + sib_recv[k].astype(F32)
+
+    right, left = lax.rem(y + 1, YS) * 2 + c, lax.rem(y + 3, YS) * 2 + c
+    far = chip_sum(0).astype(BF)
+    hops = []
+    for h, to in ((0, right), (1, left)):
+        y_send[h] = far[:, h * 256:(h + 1) * 256]
+        hops.append(pltpu.make_async_remote_copy(
+            src_ref=y_send.at[h], dst_ref=y_recv.at[h],
+            send_sem=y_send_sem.at[h], recv_sem=y_recv_sem.at[h],
+            device_id={"tp": to}, device_id_type=MESH,
+        ))
+        hops[-1].start()
+    for k in range(1, 4):
+        own_part[k] = chip_sum(k)
+    for i in range(4):
+        keys_of.step_far(i)
+    for h, to in ((0, right), (1, left)):
+        hops[h].wait_recv()
+        cols = pl.ds(h * 256, 256)
+        own_part[1 + h, :, cols] += y_recv[h].astype(F32)
+        near_send[h] = own_part[1 + h].astype(BF)
+        hops.append(pltpu.make_async_remote_copy(
+            src_ref=near_send.at[h], dst_ref=near_recv.at[h],
+            send_sem=near_send_sem.at[h], recv_sem=near_recv_sem.at[h],
+            device_id={"tp": to}, device_id_type=MESH,
+        ))
+        hops[-1].start()
+    for i in range(4):
+        keys_of.finish(i)
+    for h in range(2):
+        hops[2 + h].wait_recv()
+    mixed = (own_part[3] + near_recv[0].astype(F32) + near_recv[1].astype(F32)).astype(BF)
+    mine[...] = mixed
+    values_of.scatter(mine, True)
+    mixed_ref[...] = mixed
+
+    scale = 1.0 / math.sqrt(HS) * math.log2(math.e)
+
+    def block_of(i):
+        zq = 2 * i + (c if i % 2 == 0 else 1 - c)
+        rank = x * ZS + zq
+        return zq, rank, lax.div(rank, 2)
+
+    def chunk(buf, step):
+        return buf[lax.div(step, 4), pl.ds(lax.rem(step, 4) * 2, 2)].reshape(KEYS, HS)
+
+    def fold(op, top, s):
+        for at in range(0, KEYS, 128):
+            top = op(top, s[:, at:at + 128])
+        return top
+
+    def weigh(i):
+        zq, rank, last = block_of(i)
+        pltpu.make_async_copy(q_buf.at[i], q_buf.at[i], q_recv_sem.at[i]).wait()
+        query = q_buf[i]
+
+        def score(step, top):
+            s = nt(query, chunk(k_buf, step))
+            scores[:, pl.ds(pl.multiple_of(step * KEYS, KEYS), KEYS)] = s
+            return fold(jnp.maximum, top, s)
+
+        top = lax.fori_loop(0, last, score, jnp.full((ROWS, 128), NEG, F32))
+        s = nt(query, chunk(k_buf, last))
+        key_pos = lax.broadcasted_iota(jnp.int32, (ROWS, KEYS), 1) + last * KEYS
+        query_pos = lax.broadcasted_iota(jnp.int32, (ROWS, KEYS), 0) + rank * ROWS
+        s = jnp.where(key_pos <= query_pos, s, NEG)
+        scores[:, pl.ds(pl.multiple_of(last * KEYS, KEYS), KEYS)] = s
+        top = jnp.max(fold(jnp.maximum, top, s), axis=1, keepdims=True)
+
+        def weight(step, total):
+            cols = pl.ds(pl.multiple_of(step * KEYS, KEYS), KEYS)
+            w = jnp.exp2((scores[:, cols] - top) * scale)
+            rounded[i, :, cols] = w.astype(BF)
+            return fold(jnp.add, total, w)
+
+        total = lax.fori_loop(0, last + 1, weight, jnp.zeros((ROWS, 128), F32))
+        totals[i] = jnp.broadcast_to(jnp.sum(total, axis=1, keepdims=True), (ROWS, 128))
+
+    weigh(0)
+    for i in range(4):
+        values_of.step_own(i)
+    weigh(1)
+    for i in range(4):
+        values_of.step_near(i)
+    weigh(2)
+    for i in range(4):
+        values_of.step_far(i)
+    weigh(3)
+    for i in range(4):
+        values_of.finish(i)
+
+    def output_copies(i):
+        zq, rank, last = block_of(i)
+        core, j = lax.div(z, 4), lax.rem(z, 4)
+        alone = (zq == z) & (core == c)
+        return alone, pltpu.make_async_copy(
+            o_send.at[i], o_recv.at[j], o_recv_sem.at[j]
+        ), pltpu.make_async_remote_copy(
+            src_ref=o_send.at[i], dst_ref=o_recv.at[j],
+            send_sem=o_send_sem.at[i], recv_sem=o_recv_sem.at[j],
+            device_id={"ctx": x * ZS + zq, "tp": y * 2 + core}, device_id_type=MESH,
+        )
+
+    for i in range(4):
+        zq, rank, last = block_of(i)
+
+        def value(step, acc, i=i):
+            cols = pl.ds(pl.multiple_of(step * KEYS, KEYS), KEYS)
+            return acc + nn(rounded[i, :, cols], chunk(v_buf, step))
+
+        acc = lax.fori_loop(0, last + 1, value, jnp.zeros((ROWS, HS), F32))
+        o_send[i] = (acc / totals[i]).astype(BF)
+        alone, local, away = output_copies(i)
+        pl.when(alone)(local.start)
+        pl.when(jnp.logical_not(alone))(away.start)
+
+    keys_of.scatter(keys_ref, False)
+    values_of.scatter(mine, False)
+    for j in range(4):
+        alone, local, away = query_copies(j)
+        pl.when(jnp.logical_not(alone))(away.wait_send)
+        swaps[j].wait_send()
+        hops[j].wait_send()
+    for j in range(4):
+        pltpu.make_async_copy(o_recv.at[j], o_recv.at[j], o_recv_sem.at[j]).wait()
+        attended_ref[:, j * HS:(j + 1) * HS] = o_recv[j]
+    for i in range(4):
+        alone, local, away = output_copies(i)
+        pl.when(jnp.logical_not(alone))(away.wait_send)
+
+
+def project_and_attend(gated, out_weight, queries, keys):
+    dma = lambda *shape: pltpu.SemaphoreType.DMA(shape)
+    spread = [dma(4), dma(4), dma(4), dma(4), dma(2, 4), dma(4), dma(4)]
+    out = jax.ShapeDtypeStruct((ROWS, HEAD), BF)
+    return pl.pallas_call(
+        attend_kernel,
+        out_shape=(out, out),
+        in_specs=[pl.BlockSpec(memory_space=pltpu.VMEM)] + [pl.BlockSpec(memory_space=pl.ANY)] * 3,
+        out_specs=tuple(vmem(2)),
+        scratch_shapes=[
+            pltpu.VMEM((8, 1024, HEAD), BF),
+            pltpu.VMEM((4, ROWS, HEAD), F32),
+            pltpu.VMEM((4, ROWS, HEAD), BF),
+            pltpu.VMEM((4, ROWS, HEAD), BF),
+            pltpu.VMEM((2, ROWS, 256), BF),
+            pltpu.VMEM((2, ROWS, 256), BF),
+            pltpu.VMEM((2, ROWS, HEAD), BF),
+            pltpu.VMEM((2, ROWS, HEAD), BF),
+            pltpu.VMEM((ROWS, HEAD), BF),
+            pltpu.VMEM((XS, ZS, ROWS, HS), BF),
+            pltpu.VMEM((XS, ZS, ROWS, HS), BF),
+            pltpu.VMEM((4, ROWS, HS), BF),
+            pltpu.VMEM((ROWS, TOTAL), F32),
+            pltpu.VMEM((4, ROWS, TOTAL), BF),
+            pltpu.VMEM((4, ROWS, 128), F32),
+            pltpu.VMEM((4, ROWS, HS), BF),
+            pltpu.VMEM((4, ROWS, HS), BF),
+            dma(8), dma(4), dma(4), dma(2), dma(2), dma(2), dma(2),
+            dma(4), dma(4), dma(4), dma(4),
+        ] + spread + spread,
+        compiler_params=pltpu.CompilerParams(
+            collective_id=1, has_side_effects=True, vmem_limit_bytes=56 * 1024 * 1024
+        ),
+        name="project_and_attend",
+    )(gated, out_weight, queries, keys)
 
 
 def per_device(
     first_input, second_input, value_input, filter_taps, skip_gain, out_weight, queries, keys
 ):
-    tok_rows = first_input.shape[0]
-    gated = filtered_and_gated(
-        first_input, value_input, filter_taps, second_input, skip_gain
-    )
-    partial_sums = jnp.dot(gated, out_weight, preferred_element_type=jnp.float32)
-    mixed = lax.psum_scatter(
-        partial_sums.astype(jnp.bfloat16), "tp", scatter_dimension=1, tiled=True
-    )
-    head_count = queries.shape[1] // HS
-    score_scale = 1.0 / math.sqrt(HS)
-    ctx_rank = lax.axis_index("ctx")
-    query_pos = ctx_rank * tok_rows + jnp.arange(tok_rows, dtype=jnp.int32)
-    row_spans = ((0, tok_rows),)
-    query_heads = queries.reshape(tok_rows, head_count, HS)
-    initial = (
-        jnp.full((tok_rows, head_count), BIG_NEGATIVE, jnp.float32),
-        jnp.zeros((tok_rows, head_count), jnp.float32),
-        jnp.zeros((tok_rows, head_count, HS), jnp.float32),
-    )
-    key_piece = lax.all_gather(keys, "ctx", axis=0, tiled=True)
-    value_piece = lax.all_gather(mixed, "ctx", axis=0, tiled=True)
-    piece_rows = key_piece.shape[0]
-    key_heads = key_piece.reshape(piece_rows, head_count, HS)
-    value_heads = value_piece.reshape(piece_rows, head_count, HS)
-    key_pos = jnp.arange(piece_rows, dtype=jnp.int32)
-    span_start, span_stop = row_spans[0]
-    sub_state = (initial[0], initial[1], initial[2])
-
-    def visit(inner_state, span_start=span_start, span_stop=span_stop):
-        return fold_keys(
-            inner_state, query_heads, query_pos, key_heads, value_heads, key_pos, score_scale
-        )
-
-    def unchanged(inner_state):
-        return inner_state
-
-    sub_state = lax.cond(jnp.int32(0) <= query_pos[span_stop - 1], visit, unchanged, sub_state)
-    span_states = [sub_state]
-    top_score, weight_sum, weighted = tuple(
-        (
-            jnp.concatenate([group_state[member_index] for group_state in span_states], axis=0)
-            for member_index in range(3)
-        )
-    )
-    outcome = (
-        (weighted / weight_sum[:, :, None]).reshape(tok_rows, head_count * HS).astype(jnp.bfloat16)
-    )
-    return (mixed, outcome)
+    gated = filtered_and_gated(first_input, value_input, filter_taps, second_input, skip_gain)
+    return project_and_attend(gated, out_weight, queries, keys)
 
 
 def solution(mesh):

time: 376 us -> 136 us (0.36)
  waiting for transfers between devices: 200 us -> 0 us
  Pallas kernels: 46.8 us -> 120 us
  matrix products: 51.9 us -> 0 us
  other arithmetic: 20.8 us -> 0.02 us
  between operations: 16.1 us -> 0.68 us
  local copies, waits for them, and re-layouts: 30.3 us -> 15 us
  loops' own time: 5.36 us -> 0 us
    all_gather x2 -> x0, waiting for transfers between devices: 167 us -> none  [the longest x1 99.1 us: per_device(): value_piece = lax.all_gather(mixed, 'ctx', axis=0, tiled=True)]
    pallas_call x0 -> x1, Pallas kernels: none -> 72.8 us  [project_and_attend(): pl.pallas_call(attend_kernel, out_shape=(out, out), in_specs=[pl.BlockSpe...]
    dot_general x17 -> x0, matrix products: 51.9 us -> none  [the longest x8 27.2 us: fold_block(): jnp.einsum('qhk,khd->qhd', weights.astype(jnp.bfloat16), value_heads, pre...]
    reduce_scatter x1 -> x0, waiting for transfers between devices: 33.8 us -> none  [per_device(): lax.psum_scatter(partial_sums.astype(jnp.bfloat16), 'tp', scatter_dimensi...]
    another operation x2 -> x0, local copies, waits for them, and re-layouts: 12.2 us -> none
    add x9 -> x0, other arithmetic: 9.73 us -> none  [the longest x8 9.73 us: fold_block(): weight_sum = weight_sum * shrink + jnp.sum(weights, axis=2)]
    reduce_sum x8 -> x0, other arithmetic: 8.28 us -> none  [fold_block(): weight_sum = weight_sum * shrink + jnp.sum(weights, axis=2)]
    another operation x2 -> x0, loops' own time: 5.36 us -> none  [the longest x1 5.32 us: fold_keys(): lax.scan(scan_step, state, jnp.arange(key_rows // step_rows, dtype=jnp.in...]
  transfers between devices with their start and end apart: 3 -> 0, of which waited for: 3 -> 0; matrix products, arithmetic and copies ran while one was open for 0% -> 0% of each run, Pallas kernels for 0% -> 0%
where the time goes in v1:
time: 136 us; the launch traced here: 135 us
  Pallas kernels  120 us (88%)
  local copies, waits for them, and re-layouts  15 us (11%)
    pallas_call x1, Pallas kernels, project_and_attend(): pl.pallas_call(attend_kernel, out_shape=(out, out), in_specs=[pl.BlockSpe...  72.8 us
    pallas_call x1, Pallas kernels, filtered_and_gated(): pl.pallas_call(filter_kernel, out_shape=jax.ShapeDtypeStruct((ROWS, 1024)...  46.8 us
    unnamed x26, local copies, waits for them, and re-layouts  15 us

profile of v1, /device:TPU:6, one launch (start us, length us, event | category | flops | bytes accessed | tf_op | source)
XLA Modules:
  0.0 135.4 jit_solution(15390641846627275391)
XLA Ops:
  0.7 0.0 copy-start.1
  0.7 1.2 copy-done.1
  1.9 0.0 copy-start.2
  1.9 1.2 copy-done.2
  3.1 0.0 copy-start.3
  3.1 1.0 copy-done.3
  4.2 0.0 copy-start.4
  4.2 1.0 copy-done.4
  5.2 1.0 copy-done.5
  6.2 0.0 copy-start.6
  6.2 1.0 copy-done.6
  7.3 0.0 copy-start.7
  7.3 1.0 copy-done.7
  8.3 0.0 copy-start.8
  8.3 1.0 copy-done.8
  9.4 0.8 copy-done.9
  10.1 0.8 copy-done.10
  10.9 0.7 copy-done.11
  11.6 46.8 %filter_and_gate.1.gated_ref = bf16[256,1024]{1,0:T(8,128)(2,1)S(1)} custom-call(bf16[256,1024]{1,0:T(8,128)(2,1)S(1)} %copy-done.3, bf16[256,1024]{1,0:T(8,128)(2,1)S(1)} %copy-done.4, bf16[256,1024]{1,0:T(8,128)(2,1)S(1)} %copy-done.5, bf16[256,1024]{1,0:T(8,128)(2,1)S(1)} %copy-done.6, f32[1,1024]{1,0:T(1,128)S(1)} %bitcast.1, ...), custom_call_target="tpu_custom_call" | custom-call | tf_op jit(solution)/shard_map/filter_and_gate/pallas_call | solution.py:156
  58.4 0.0 copy-start
  58.4 0.8 copy-done
  59.2 72.8 %project_and_attend.1 = (bf16[256,512]{1,0:T(8,128)(2,1)}, bf16[256,512]{1,0:T(8,128)(2,1)}) custom-call(bf16[256,1024]{1,0:T(8,128)(2,1)} %copy-done, bf16[1024,4096]{1,0:T(8,128)(2,1)} %weight_ref.1, bf16[256,512]{1,0:T(8,128)(2,1)} %queries_ref.1, bf16[256,512]{1,0:T(8,128)(2,1)} %keys_ref.1), custom_call_target="tpu_custom_call" | custom-call | tf_op jit(solution)/shard_map/project_and_attend/pallas_call | solution.py:475
  132.0 1.7 %copy.18 = bf16[256,512]{1,0:T(8,128)(2,1)} copy(bf16[256,512]{1,0:T(8,128)(2,1)} %get-tuple-element.4) | data formatting | bytes 524288
  133.7 1.7 %copy.19 = bf16[256,512]{1,0:T(8,128)(2,1)} copy(bf16[256,512]{1,0:T(8,128)(2,1)} %get-tuple-element.5) | data formatting | bytes 524288
  (5 shorter events, 0.0 us)
Async XLA Ops:
  0.7 1.2 copy-start.1
  1.9 1.2 copy-start.2
  3.1 1.0 copy-start.3
  4.2 1.0 copy-start.4
  5.2 1.0 copy-start.5
  6.2 1.0 copy-start.6
  7.3 1.0 copy-start.7
  8.3 1.0 copy-start.8
  9.4 0.8 copy-start.9
  10.1 0.8 copy-start.10
  10.9 0.7 copy-start.11
  58.4 0.8 copy-start

commit v2 on v1

v2 whole, which is shorter than its diff:
```python
import functools
import math

import jax
import jax.numpy as jnp
import numpy as np
from jax import lax
from jax.experimental import pallas as pl
from jax.experimental.pallas import tpu as pltpu
from jax.sharding import PartitionSpec as P

HS = 128
MESH = pl.DeviceIdType.MESH
BF = jnp.bfloat16
F32 = jnp.float32
CTX = 32
ROWS = 256
GROUP = 16
TOTAL = CTX * ROWS


def nt(a, b):
    return lax.dot_general(a, b, (((1,), (1,)), ((), ())), preferred_element_type=F32)


def nn(a, b):
    return jnp.dot(a, b, preferred_element_type=F32)


def tables():
    r = np.arange(CTX, dtype=np.float64)
    q = np.arange(CTX, dtype=np.float64)
    a = np.arange(ROWS, dtype=np.float64)
    rows = np.exp(-2j * np.pi * np.outer(q + 0.25, r) / CTX)
    turn = np.exp(-2j * np.pi * np.outer(q + 0.25, a) / TOTAL)
    cols = np.exp(-2j * np.pi * np.outer(a, a) / ROWS)
    eye = np.eye(GROUP)
    spread = lambda m: np.einsum("qr,cd->cqrd", m, eye).reshape(GROUP * CTX, CTX * GROUP)
    first = np.concatenate([spread(rows.real), spread(rows.imag)], axis=0)
    back = np.conj(rows).T
    gather = lambda m: np.einsum("rq,cd->rcdq", m, eye).reshape(CTX * GROUP, GROUP * CTX)
    last = np.concatenate([gather(back.real), -gather(back.imag)], axis=1)
    mix = np.block([[cols.real, cols.imag], [-cols.imag, cols.real]])
    unmix = np.block([[cols.real, -cols.imag], [cols.imag, cols.real]]) / TOTAL
    cast = lambda m: np.asarray(m, np.float32).astype(jnp.bfloat16)
    return (cast(first), cast(mix), cast(unmix), cast(last),
            np.asarray(turn.real, np.float32), np.asarray(turn.imag, np.float32))


def spectrum(x, first, mix, turn_re, turn_im):
    half = GROUP * CTX
    a = nn(first, x)
    a_re = a[:half].reshape(GROUP, CTX, ROWS)
    a_im = a[half:].reshape(GROUP, CTX, ROWS)
    z_re = (a_re * turn_re - a_im * turn_im).reshape(half, ROWS).astype(BF)
    z_im = (a_re * turn_im + a_im * turn_re).reshape(half, ROWS).astype(BF)
    return nn(jnp.concatenate([z_re, z_im], axis=1), mix)


XS, ZS, YS = 4, 8, 4
HEAD = 512
KEYS = 512
NEG = -1e30


class Spread:
    def __init__(self, place, buf, z_send, own, left, right, far, sib, sent):
        self.x, self.z, self.y, self.c = place
        self.buf, self.z_send, self.own, self.left, self.right, self.far, self.sib, self.sent = (
            buf, z_send, own, left, right, far, sib, sent
        )
        self.xl, self.xr, self.x2 = (lax.rem(self.x + k, XS) for k in (3, 1, 2))

    def device(self, x, z, c):
        return {"ctx": x * ZS + z, "tp": self.y * 2 + c}

    def scatter(self, source, start):
        x, z, c = self.x, self.z, self.c
        core, i = lax.rem(z, 2), lax.div(z, 2)
        for j in range(4):
            to = 4 * c + j
            alone = (to == z) & (core == c)
            part = source.at[:, pl.ds(j * HS, HS)]
            slot = self.buf.at[x, z]
            local = lambda: pltpu.make_async_copy(part, slot, self.own.at[i])
            away = lambda: pltpu.make_async_remote_copy(
                src_ref=part, dst_ref=slot, send_sem=self.z_send.at[j], recv_sem=self.own.at[i],
                device_id=self.device(x, to, core), device_id_type=MESH,
            )
            if start:
                start_either(alone, local, away)
            else:
                pl.when(jnp.logical_not(alone))(lambda: away().wait_send())

    def push(self, block, i, x, c, sem):
        pltpu.make_async_remote_copy(
            src_ref=block, dst_ref=block, send_sem=self.sent.at[i], recv_sem=sem,
            device_id=self.device(x, self.z, c), device_id_type=MESH,
        ).start()

    def arrived(self, block, sem):
        pltpu.make_async_copy(block, block, sem).wait()

    def step_own(self, i):
        block = self.buf.at[self.x, 2 * i + self.c]
        self.arrived(block, self.own.at[i])
        self.push(block, i, self.xr, self.c, self.left.at[i])
        self.push(block, i, self.xl, self.c, self.right.at[i])
        self.push(block, i, self.x, 1 - self.c, self.sib.at[i])

    def step_near(self, i):
        zi = 2 * i + self.c
        block = self.buf.at[self.xl, zi]
        self.arrived(block, self.left.at[i])
        half = self.buf.at[self.xl, zi, pl.ds(0, 128)]
        self.push(half, i, self.xr, self.c, self.far.at[0, i])
        self.push(block, i, self.x, 1 - self.c, self.sib.at[i])
        block = self.buf.at[self.xr, zi]
        self.arrived(block, self.right.at[i])
        half = self.buf.at[self.xr, zi, pl.ds(128, 128)]
        self.push(half, i, self.xl, self.c, self.far.at[1, i])
        self.push(block, i, self.x, 1 - self.c, self.sib.at[i])

    def step_far(self, i):
        for h in range(2):
            half = self.buf.at[self.x2, 2 * i + self.c, pl.ds(h * 128, 128)]
            self.arrived(half, self.far.at[h, i])
            self.push(half, i, self.x, 1 - self.c, self.sib.at[i])

    def finish(self, i):
        blocks = self.buf.at[:, 2 * i + 1 - self.c]
        self.arrived(blocks, self.sib.at[i])
        some = self.buf.at[0, pl.ds(0, 7)]
        self.arrived(some, self.sent.at[i])

CHUNKS = 36


def whole_kernel(
    first_hbm, second_hbm, value_hbm, taps_hbm, skip_hbm, weight_ref, queries_ref, keys_ref,
    spread_hbm, mix_hbm, unmix_hbm, gather_hbm, turn_hbm, mixed_ref, attended_ref,
    first_in, value_in, taps_in, second_in, skip, spread_t, mix_t, unmix_t, gather_t, turn,
    product, send, recv, out_send, out_recv, gated_ref,
    weights, own_part, sib_send, sib_recv, y_send, y_recv, near_send, near_recv, mine,
    k_buf, v_buf, q_buf, scores, rounded, totals, o_send, o_recv,
    in_sem, table_sem, send_sem, recv_sem, back_send_sem, back_recv_sem,
    w_sem, sib_send_sem, sib_recv_sem, y_send_sem, y_recv_sem, near_send_sem, near_recv_sem,
    q_send_sem, q_recv_sem, o_send_sem, o_recv_sem,
    kz, k_own, k_left, k_right, k_far, k_sib, k_sent,
    vz, v_own, v_left, v_right, v_far, v_sib, v_sent,
):
    me, tp = lax.axis_index("ctx"), lax.axis_index("tp")
    x, z = lax.div(me, ZS), lax.rem(me, ZS)
    y, c = lax.div(tp, 2), lax.rem(tp, 2)
    place = (x, z, y, c)
    keys_of = Spread(place, k_buf, kz, k_own, k_left, k_right, k_far, k_sib, k_sent)
    values_of = Spread(place, v_buf, vz, v_own, v_left, v_right, v_far, v_sib, v_sent)
    mirror = XS - 1 - x
    half = GROUP * CTX

    line = [lax.rem(x + s, XS) for s in range(4)]
    cols_of = [pl.ds(pl.multiple_of(at * 256, 256), 256) for at in line]
    inputs = []
    for s in range(4):
        for k, (hbm, into) in enumerate(
            ((taps_hbm, taps_in), (first_hbm, first_in), (value_hbm, value_in))
        ):
            inputs.append(pltpu.make_async_copy(hbm.at[:, cols_of[s]], into.at[s], in_sem.at[k, s]))
            inputs[-1].start()

    barrier = pltpu.get_barrier_semaphore()

    def greet(to_ctx, to_tp):
        pl.semaphore_signal(
            barrier, inc=1, device_id={"ctx": to_ctx, "tp": to_tp}, device_id_type=MESH
        )

    def greet_group(k, carry):
        greet(lax.rem(me + k, CTX), tp)
        return carry

    def greet_rows(k, carry):
        greet(x * ZS + k, y * 2 + 1 - c)
        greet(mirror * ZS + k, y * 2 + 1 - c)
        return carry

    lax.fori_loop(1, CTX, greet_group, 0)
    lax.fori_loop(0, ZS, greet_rows, 0)
    for k in (1, 3):
        greet(me, lax.rem(y + k, YS) * 2 + c)

    tables_in = []
    for k, (hbm, into) in enumerate((
        (spread_hbm, spread_t), (turn_hbm, turn), (mix_hbm, mix_t), (unmix_hbm, unmix_t),
        (gather_hbm, gather_t), (skip_hbm, skip),
    )):
        tables_in.append(pltpu.make_async_copy(hbm, into, table_sem.at[k]))
        tables_in[-1].start()
    gates_in = []
    for s in range(4):
        gates_in.append(
            pltpu.make_async_copy(second_hbm.at[:, cols_of[s]], second_in.at[s], in_sem.at[3, s])
        )
        gates_in[-1].start()

    def post(h, s, k):
        zt = lax.rem(z + k, ZS)
        pltpu.make_async_remote_copy(
            src_ref=send.at[h, s, zt], dst_ref=recv.at[h, me],
            send_sem=send_sem.at[h], recv_sem=recv_sem.at[h],
            device_id={"ctx": line[s] * ZS + zt}, device_id_type=MESH,
        ).start()

    def post_line(h, s):
        def one(k, carry):
            post(h, s, k)
            return carry

        if s == 0:
            pltpu.make_async_copy(send.at[h, 0, z], recv.at[h, me], recv_sem.at[h]).start()
        lax.fori_loop(1 if s == 0 else 0, ZS, one, 0)

    def same(rows):
        down = lax.broadcasted_iota(jnp.int32, (rows, rows), 0)
        across = lax.broadcasted_iota(jnp.int32, (rows, rows), 1)
        return jnp.where(down == across, 1.0, 0.0).astype(BF)

    eye = same(ROWS)
    for s in range(4):
        for copy in inputs[3 * s:3 * s + 3]:
            copy.wait()
        prod = (first_in[s].astype(F32) * value_in[s].astype(F32)).astype(BF)
        product[s] = prod
        for kind, block in ((0, prod), (1, taps_in[s])):
            turned = nt(eye, block).astype(BF)
            for dl in range(8):
                for h in range(2):
                    at = dl * 32 + h * GROUP
                    send[h, s, dl, kind] = turned[at:at + GROUP]
        if s == 0:
            pl.semaphore_wait(barrier, CTX - 1 + 2 * ZS + 2)
        post_line(0, s)
    for s in range(4):
        post_line(1, s)

    order = [(other, lax.rem(y + k, YS)) for other in (1, 0) for k in (2, 1, 3, 0)]
    loads = []
    for k, (other, to_y) in enumerate(order):
        col = to_y * 2 + (1 - c if other else c)
        loads.append(pltpu.make_async_copy(
            weight_ref.at[:, pl.ds(pl.multiple_of(col * HEAD, HEAD), HEAD)], weights.at[k], w_sem.at[k]
        ))
        loads[-1].start()
    for copy in tables_in:
        copy.wait()

    for h in range(2):
        pltpu.make_async_copy(recv.at[h], recv.at[h], recv_sem.at[h]).wait()
        tr, ti = turn[:CTX], turn[CTX:]
        xs = recv[h, :, 0].reshape(half, ROWS)
        ws = recv[h, :, 1].reshape(half, ROWS)
        d = spectrum(xs, spread_t[...], mix_t[...], tr, ti)
        e = spectrum(ws, spread_t[...], mix_t[...], tr, ti)
        d_re, d_im, e_re, e_im = d[:, :ROWS], d[:, ROWS:], e[:, :ROWS], e[:, ROWS:]
        y_re = (d_re * e_re - d_im * e_im).astype(BF)
        y_im = (d_re * e_im + d_im * e_re).astype(BF)
        b = nn(jnp.concatenate([y_re, y_im], axis=1), unmix_t[...])
        b_re = b[:, :ROWS].reshape(GROUP, CTX, ROWS)
        b_im = b[:, ROWS:].reshape(GROUP, CTX, ROWS)
        c_re = (b_re * tr + b_im * ti).reshape(half, ROWS).astype(BF)
        c_im = (b_im * tr - b_re * ti).reshape(half, ROWS).astype(BF)
        out = nn(gather_t[...], jnp.concatenate([c_re, c_im], axis=0))
        out_send[h] = out.astype(BF).reshape(CTX, GROUP, ROWS)

        def reply(k, carry, h=h):
            to = lax.rem(me + k, CTX)
            pltpu.make_async_remote_copy(
                src_ref=out_send.at[h, to], dst_ref=out_recv.at[h, me],
                send_sem=back_send_sem.at[h], recv_sem=back_recv_sem.at[h],
                device_id={"ctx": to}, device_id_type=MESH,
            ).start()
            return carry

        pltpu.make_async_copy(out_send.at[h, me], out_recv.at[h, me], back_recv_sem.at[h]).start()
        lax.fori_loop(1, CTX, reply, 0)

    for copy in gates_in:
        copy.wait()
    for h in range(2):
        pltpu.make_async_copy(out_recv.at[h], out_recv.at[h], back_recv_sem.at[h]).wait()

    keys_of.scatter(keys_ref, True)
    far_pair = lax.min(z, ZS - 1 - z)
    q_x = lax.select(far_pair < 2, x, mirror)
    q_core = lax.rem(far_pair, 2)
    q_slot = lax.div(far_pair, 2) * 2 + lax.div(z, 4)

    def query_copies(j):
        to = 4 * c + j
        alone = (to == z) & (q_core == c) & (far_pair < 2)
        part = queries_ref.at[:, pl.ds(j * HS, HS)]
        slot = q_buf.at[q_slot]
        sem = q_recv_sem.at[q_slot]
        local = lambda: pltpu.make_async_copy(part, slot, sem)
        away = lambda: pltpu.make_async_remote_copy(
            src_ref=part, dst_ref=slot, send_sem=q_send_sem.at[j], recv_sem=sem,
            device_id={"ctx": q_x * ZS + to, "tp": y * 2 + q_core}, device_id_type=MESH,
        )
        return alone, local, away

    for j in range(4):
        start_either(*query_copies(j))

    for s in range(4):
        parts = [out_recv[h, line[s] * 8 + dl] for dl in range(8) for h in range(2)]
        filtered = nt(eye, jnp.concatenate(parts, axis=0)).astype(BF).astype(F32)
        gated_ref[:, cols_of[s]] = (
            second_in[s].astype(F32) * (filtered + skip[:, cols_of[s]] * product[s].astype(F32))
        ).astype(BF)

    gated = gated_ref[...]
    swaps = []
    for k in range(4):
        loads[k].wait()
        sib_send[k] = nn(gated, weights[k]).astype(BF)
        swaps.append(pltpu.make_async_remote_copy(
            src_ref=sib_send.at[k], dst_ref=sib_recv.at[k],
            send_sem=sib_send_sem.at[k], recv_sem=sib_recv_sem.at[k],
            device_id={"tp": y * 2 + 1 - c}, device_id_type=MESH,
        ))
        swaps[-1].start()
    for k in range(4):
        loads[4 + k].wait()
        own_part[k] = nn(gated, weights[4 + k])

    def chip_sum(k):
        swaps[k].wait_recv()
        return own_part[k] + sib_recv[k].astype(F32)

    right, left = lax.rem(y + 1, YS) * 2 + c, lax.rem(y + 3, YS) * 2 + c
    far = chip_sum(0).astype(BF)
    hops = []
    for h, to in ((0, right), (1, left)):
        y_send[h] = far[:, h * 256:(h + 1) * 256]
        hops.append(pltpu.make_async_remote_copy(
            src_ref=y_send.at[h], dst_ref=y_recv.at[h],
            send_sem=y_send_sem.at[h], recv_sem=y_recv_sem.at[h],
            device_id={"tp": to}, device_id_type=MESH,
        ))
        hops[-1].start()
    for k in range(1, 4):
        own_part[k] = chip_sum(k)
    for i in range(4):
        keys_of.step_own(i)
    for h, to in ((0, right), (1, left)):
        hops[h].wait_recv()
        cols = pl.ds(h * 256, 256)
        own_part[1 + h, :, cols] += y_recv[h].astype(F32)
        near_send[h] = own_part[1 + h].astype(BF)
        hops.append(pltpu.make_async_remote_copy(
            src_ref=near_send.at[h], dst_ref=near_recv.at[h],
            send_sem=near_send_sem.at[h], recv_sem=near_recv_sem.at[h],
            device_id={"tp": to}, device_id_type=MESH,
        ))
        hops[-1].start()
    for i in range(4):
        keys_of.step_near(i)
    for h in range(2):
        hops[2 + h].wait_recv()
    mixed = (own_part[3] + near_recv[0].astype(F32) + near_recv[1].astype(F32)).astype(BF)
    mine[...] = mixed
    values_of.scatter(mine, True)
    mixed_ref[...] = mixed
    for i in range(4):
        keys_of.step_far(i)
    for i in range(4):
        keys_of.finish(i)

    scale = 1.0 / math.sqrt(HS) * math.log2(math.e)
    blocks, first_step = [], []
    steps_before = 0
    for i in range(4):
        row = x if i < 2 else mirror
        pair = c + 2 * (i // 2)
        zq = pair if i % 2 == 0 else ZS - 1 - pair
        rank = row * ZS + zq
        blocks.append((row, zq, rank, lax.div(rank, 2)))
        first_step.append(steps_before)
        steps_before = steps_before + lax.div(rank, 2) + 1

    def chunk(buf, step):
        return buf[lax.div(step, 4), pl.ds(lax.rem(step, 4) * 2, 2)].reshape(KEYS, HS)

    def fold(op, top, s):
        for at in range(0, KEYS, 128):
            top = op(top, s[:, at:at + 128])
        return top

    def weigh(i):
        row, zq, rank, last = blocks[i]
        pltpu.make_async_copy(q_buf.at[i], q_buf.at[i], q_recv_sem.at[i]).wait()
        query = q_buf[i]

        def score(step, top):
            s = nt(query, chunk(k_buf, step))
            scores[step] = s
            return fold(jnp.maximum, top, s)

        top = lax.fori_loop(0, last, score, jnp.full((ROWS, 128), NEG, F32))
        s = nt(query, chunk(k_buf, last))
        key_pos = lax.broadcasted_iota(jnp.int32, (ROWS, KEYS), 1) + last * KEYS
        query_pos = lax.broadcasted_iota(jnp.int32, (ROWS, KEYS), 0) + rank * ROWS
        s = jnp.where(key_pos <= query_pos, s, NEG)
        scores[last] = s
        top = jnp.max(fold(jnp.maximum, top, s), axis=1, keepdims=True)

        def weight(step, total):
            w = jnp.exp2((scores[step] - top) * scale)
            rounded[first_step[i] + step] = w.astype(BF)
            return fold(jnp.add, total, w)

        total = lax.fori_loop(0, last + 1, weight, jnp.zeros((ROWS, 128), F32))
        totals[i] = jnp.broadcast_to(jnp.sum(total, axis=1, keepdims=True), (ROWS, 128))

    weigh(0)
    weigh(1)
    for i in range(4):
        values_of.step_own(i)
    weigh(2)
    weigh(3)
    for i in range(4):
        values_of.step_near(i)
    for i in range(4):
        values_of.step_far(i)
    for i in range(4):
        values_of.finish(i)

    def output_copies(i):
        row, zq, rank, last = blocks[i]
        core, j = lax.div(z, 4), lax.rem(z, 4)
        alone = (zq == z) & (core == c) & (row == x)
        local = lambda: pltpu.make_async_copy(o_send.at[i], o_recv.at[j], o_recv_sem.at[j])
        away = lambda: pltpu.make_async_remote_copy(
            src_ref=o_send.at[i], dst_ref=o_recv.at[j],
            send_sem=o_send_sem.at[i], recv_sem=o_recv_sem.at[j],
            device_id={"ctx": row * ZS + zq, "tp": y * 2 + core}, device_id_type=MESH,
        )
        return alone, local, away

    for i in range(4):
        row, zq, rank, last = blocks[i]

        def value(step, acc, i=i):
            return acc + nn(rounded[first_step[i] + step], chunk(v_buf, step))

        acc = lax.fori_loop(0, last + 1, value, jnp.zeros((ROWS, HS), F32))
        o_send[i] = (acc / totals[i]).astype(BF)
        start_either(*output_copies(i))

    for h in range(2):
        some = recv.at[h, pl.ds(0, CTX - 1)]
        pltpu.make_async_copy(some, some, send_sem.at[h]).wait()
        some = out_recv.at[h, pl.ds(0, CTX - 1)]
        pltpu.make_async_copy(some, some, back_send_sem.at[h]).wait()
    keys_of.scatter(keys_ref, False)
    values_of.scatter(mine, False)
    for j in range(4):
        alone, local, away = query_copies(j)
        pl.when(jnp.logical_not(alone))(lambda away=away: away().wait_send())
        swaps[j].wait_send()
        hops[j].wait_send()
    for j in range(4):
        pltpu.make_async_copy(o_recv.at[j], o_recv.at[j], o_recv_sem.at[j]).wait()
        attended_ref[:, j * HS:(j + 1) * HS] = o_recv[j]
    for i in range(4):
        alone, local, away = output_copies(i)
        pl.when(jnp.logical_not(alone))(lambda away=away: away().wait_send())


def start_either(alone, local, away):
    pl.when(alone)(lambda: local().start())
    pl.when(jnp.logical_not(alone))(lambda: away().start())


def vmem(count):
    return [pl.BlockSpec(memory_space=pltpu.VMEM)] * count


def hbm(count):
    return [pl.BlockSpec(memory_space=pl.ANY)] * count


def hand_over(a, b, a_out, b_out, sem):
    copies = [
        pltpu.make_async_copy(a, a_out, sem.at[0]),
        pltpu.make_async_copy(b, b_out, sem.at[1]),
    ]
    for copy in copies:
        copy.start()
    for copy in copies:
        copy.wait()


def per_device(
    first_input, second_input, value_input, filter_taps, skip_gain, out_weight, queries, keys
):
    spread, mix, unmix, gather, turn_re, turn_im = tables()
    consts = [jnp.asarray(t) for t in (spread, mix, unmix, gather, np.concatenate([turn_re, turn_im]))]
    dma = lambda *shape: pltpu.SemaphoreType.DMA(shape)
    bf = lambda *shape: pltpu.VMEM(shape, BF)
    fl = lambda *shape: pltpu.VMEM(shape, F32)
    sems = [dma(4), dma(4), dma(4), dma(4), dma(2, 4), dma(4), dma(4)]
    out = jax.ShapeDtypeStruct((ROWS, HEAD), BF)
    mixed, attended = pl.pallas_call(
        whole_kernel,
        out_shape=(out, out),
        in_specs=hbm(13),
        out_specs=tuple(vmem(2)),
        scratch_shapes=[
            bf(4, ROWS, 256), bf(4, ROWS, 256), bf(4, ROWS, 256), bf(4, ROWS, 256),
            fl(1, 1024), bf(1024, 512), bf(512, 512), bf(512, 512), bf(512, 1024), fl(2 * CTX, ROWS),
            bf(4, ROWS, 256),
            bf(2, 4, 8, 2, GROUP, ROWS), bf(2, CTX, 2, GROUP, ROWS),
            bf(2, CTX, GROUP, ROWS), bf(2, CTX, GROUP, ROWS),
            bf(ROWS, 1024),
            bf(8, 1024, HEAD), fl(4, ROWS, HEAD), bf(4, ROWS, HEAD), bf(4, ROWS, HEAD),
            bf(2, ROWS, 256), bf(2, ROWS, 256), bf(2, ROWS, HEAD), bf(2, ROWS, HEAD), bf(ROWS, HEAD),
            bf(XS, ZS, ROWS, HS), bf(XS, ZS, ROWS, HS), bf(4, ROWS, HS),
            fl(TOTAL // KEYS, ROWS, KEYS), bf(CHUNKS, ROWS, KEYS), fl(4, ROWS, 128),
            bf(4, ROWS, HS), bf(4, ROWS, HS),
            dma(4, 4), dma(6), dma(2), dma(2), dma(2), dma(2),
            dma(8), dma(4), dma(4), dma(2), dma(2), dma(2), dma(2),
            dma(4), dma(4), dma(4), dma(4),
        ] + sems + sems,
        compiler_params=pltpu.CompilerParams(
            collective_id=0, has_side_effects=True, vmem_limit_bytes=60 * 1024 * 1024
        ),
        name="whole",
    )(first_input, second_input, value_input, filter_taps, skip_gain.reshape(1, 1024), out_weight,
      queries, keys, *consts)
    return pl.pallas_call(
        hand_over,
        out_shape=(out, out),
        in_specs=hbm(2),
        out_specs=tuple(hbm(2)),
        scratch_shapes=[dma(2)],
        name="hand_over",
    )(mixed, attended)


def solution(mesh):
    return jax.shard_map(
        per_device,
        mesh=mesh,
        in_specs=(
            P("ctx", "tp"),
            P("ctx", "tp"),
            P("ctx", "tp"),
            P("ctx", "tp"),
            P("tp"),
            P("tp", None),
            P("ctx", "tp"),
            P("ctx", "tp"),
        ),
        out_specs=(P("ctx", "tp"), P("ctx", "tp")),
        check_vma=False,
    )
```

time: 136 us -> 127 us (0.934)
  the two profiles are of different devices: /device:TPU:6 before, /device:TPU:121 now
where the time goes in v2:
time: 127 us
  Pallas kernels  126 us (99%)
    pallas_call x1, Pallas kernels, per_device(): pl.pallas_call(whole_kernel, out_shape=(out, out), in_specs=hbm(13), out_...  109 us
    pallas_call x1, Pallas kernels, per_device(): pl.pallas_call(hand_over, out_shape=(out, out), in_specs=hbm(2), out_spec...  17 us

profile of v2, /device:TPU:121, one launch (start us, length us, event | category | flops | bytes accessed | tf_op | source)
XLA Modules:
  0.0 127.0 jit_solution(3432397243621163000)
XLA Ops:
  0.6 109.4 %whole.1 = (bf16[256,512]{1,0:T(8,128)(2,1)}, bf16[256,512]{1,0:T(8,128)(2,1)}) custom-call(bf16[256,1024]{1,0:T(8,128)(2,1)} %first_hbm.1, bf16[256,1024]{1,0:T(8,128)(2,1)} %second_hbm.1, bf16[256,1024]{1,0:T(8,128)(2,1)} %value_hbm.1, bf16[256,1024]{1,0:T(8,128)(2,1)} %taps_hbm.1, f32[1,1024]{1,0:T(1,128)} %bitcast.1, bf16[1024,4096]{1,0:T(8,128)(2,1)} %weight_ref.1, ...), custom_call_target="tpu_custom_call" | custom-call | tf_op jit(solution)/shard_map/whole/pallas_call | solution.py:514
  110.0 17.0 %hand_over.1 = (bf16[256,512]{1,0:T(8,128)(2,1)}, bf16[256,512]{1,0:T(8,128)(2,1)}) custom-call(bf16[256,512]{1,0:T(8,128)(2,1)} %get-tuple-element.4.a, bf16[256,512]{1,0:T(8,128)(2,1)} %get-tuple-element.5.b), custom_call_target="tpu_custom_call" | custom-call | tf_op jit(solution)/shard_map/hand_over/pallas_call | solution.py:541

commit v3 on v2

--- a/solution.py
+++ b/solution.py
@@ -64,27 +64,31 @@
 
 
 class Spread:
-    def __init__(self, place, buf, z_send, own, left, right, far, sib, sent):
+    def __init__(self, place, buf, parts, z_send, own, left, right, far, sib, sent):
         self.x, self.z, self.y, self.c = place
         self.buf, self.z_send, self.own, self.left, self.right, self.far, self.sib, self.sent = (
             buf, z_send, own, left, right, far, sib, sent
         )
+        self.rows = ROWS // parts
         self.xl, self.xr, self.x2 = (lax.rem(self.x + k, XS) for k in (3, 1, 2))
 
     def device(self, x, z, c):
         return {"ctx": x * ZS + z, "tp": self.y * 2 + c}
 
-    def scatter(self, source, start):
+    def span(self, p):
+        return pl.ds(p * self.rows, self.rows)
+
+    def scatter(self, source, p, start):
         x, z, c = self.x, self.z, self.c
-        core, i = lax.rem(z, 2), lax.div(z, 2)
+        core = lax.rem(z, 2)
         for j in range(4):
             to = 4 * c + j
             alone = (to == z) & (core == c)
-            part = source.at[:, pl.ds(j * HS, HS)]
-            slot = self.buf.at[x, z]
-            local = lambda: pltpu.make_async_copy(part, slot, self.own.at[i])
+            part = source.at[self.span(p), pl.ds(j * HS, HS)]
+            slot = self.buf.at[x, core, lax.div(z, 2), self.span(p)]
+            local = lambda: pltpu.make_async_copy(part, slot, self.own.at[p])
             away = lambda: pltpu.make_async_remote_copy(
-                src_ref=part, dst_ref=slot, send_sem=self.z_send.at[j], recv_sem=self.own.at[i],
+                src_ref=part, dst_ref=slot, send_sem=self.z_send.at[p, j], recv_sem=self.own.at[p],
                 device_id=self.device(x, to, core), device_id_type=MESH,
             )
             if start:
@@ -92,47 +96,48 @@
             else:
                 pl.when(jnp.logical_not(alone))(lambda: away().wait_send())
 
-    def push(self, block, i, x, c, sem):
+    def push(self, block, p, x, c, sem, late=1):
         pltpu.make_async_remote_copy(
-            src_ref=block, dst_ref=block, send_sem=self.sent.at[i], recv_sem=sem,
+            src_ref=block, dst_ref=block, send_sem=self.sent.at[late, p], recv_sem=sem,
             device_id=self.device(x, self.z, c), device_id_type=MESH,
         ).start()
 
     def arrived(self, block, sem):
         pltpu.make_async_copy(block, block, sem).wait()
 
-    def step_own(self, i):
-        block = self.buf.at[self.x, 2 * i + self.c]
-        self.arrived(block, self.own.at[i])
-        self.push(block, i, self.xr, self.c, self.left.at[i])
-        self.push(block, i, self.xl, self.c, self.right.at[i])
-        self.push(block, i, self.x, 1 - self.c, self.sib.at[i])
-
-    def step_near(self, i):
-        zi = 2 * i + self.c
-        block = self.buf.at[self.xl, zi]
-        self.arrived(block, self.left.at[i])
-        half = self.buf.at[self.xl, zi, pl.ds(0, 128)]
-        self.push(half, i, self.xr, self.c, self.far.at[0, i])
-        self.push(block, i, self.x, 1 - self.c, self.sib.at[i])
-        block = self.buf.at[self.xr, zi]
-        self.arrived(block, self.right.at[i])
-        half = self.buf.at[self.xr, zi, pl.ds(128, 128)]
-        self.push(half, i, self.xl, self.c, self.far.at[1, i])
-        self.push(block, i, self.x, 1 - self.c, self.sib.at[i])
-
-    def step_far(self, i):
+    def step_own(self, p):
+        block = self.buf.at[self.x, self.c, :, self.span(p)]
+        self.arrived(block, self.own.at[p])
+        self.push(block, p, self.xr, self.c, self.left.at[p], 0)
+        self.push(block, p, self.xl, self.c, self.right.at[p], 0)
+        self.push(block, p, self.x, 1 - self.c, self.sib.at[self.x, p], 0)
+
+    def half(self, x, p, h):
+        return self.buf.at[x, self.c, :, pl.ds(p * self.rows + h * (self.rows // 2), self.rows // 2)]
+
+    def step_near(self, p):
+        for h, x, on, sem in ((0, self.xl, self.xr, self.left), (1, self.xr, self.xl, self.right)):
+            block = self.buf.at[x, self.c, :, self.span(p)]
+            self.arrived(block, sem.at[p])
+            self.push(self.half(x, p, h), p, on, self.c, self.far.at[h, p])
+            self.push(block, p, self.x, 1 - self.c, self.sib.at[x, p])
+
+    def step_far(self, p):
         for h in range(2):
-            half = self.buf.at[self.x2, 2 * i + self.c, pl.ds(h * 128, 128)]
-            self.arrived(half, self.far.at[h, i])
-            self.push(half, i, self.x, 1 - self.c, self.sib.at[i])
-
-    def finish(self, i):
-        blocks = self.buf.at[:, 2 * i + 1 - self.c]
-        self.arrived(blocks, self.sib.at[i])
-        some = self.buf.at[0, pl.ds(0, 7)]
-        self.arrived(some, self.sent.at[i])
-
+            half = self.half(self.x2, p, h)
+            self.arrived(half, self.far.at[h, p])
+            self.push(half, p, self.x, 1 - self.c, self.sib.at[self.x2, p])
+
+    def finish(self, p):
+        for x in range(XS):
+            self.arrived(self.buf.at[x, 1 - self.c, :, self.span(p)], self.sib.at[x, p])
+
+    def drain(self, p):
+        self.arrived(self.buf.at[pl.ds(0, 3), 0, :, self.span(p)], self.sent.at[0, p])
+        self.arrived(self.buf.at[:, 0, :, self.span(p)], self.sent.at[1, p])
+
+
+PARTS = 2
 CHUNKS = 36
 
 
@@ -153,8 +158,8 @@
     x, z = lax.div(me, ZS), lax.rem(me, ZS)
     y, c = lax.div(tp, 2), lax.rem(tp, 2)
     place = (x, z, y, c)
-    keys_of = Spread(place, k_buf, kz, k_own, k_left, k_right, k_far, k_sib, k_sent)
-    values_of = Spread(place, v_buf, vz, v_own, v_left, v_right, v_far, v_sib, v_sent)
+    keys_of = Spread(place, k_buf, 1, kz, k_own, k_left, k_right, k_far, k_sib, k_sent)
+    values_of = Spread(place, v_buf, PARTS, vz, v_own, v_left, v_right, v_far, v_sib, v_sent)
     mirror = XS - 1 - x
     half = GROUP * CTX
 
@@ -235,13 +240,14 @@
             turned = nt(eye, block).astype(BF)
             for dl in range(8):
                 for h in range(2):
-                    at = dl * 32 + h * GROUP
+                    at = h * 128 + dl * GROUP
                     send[h, s, dl, kind] = turned[at:at + GROUP]
         if s == 0:
             pl.semaphore_wait(barrier, CTX - 1 + 2 * ZS + 2)
         post_line(0, s)
     for s in range(4):
         post_line(1, s)
+    keys_of.scatter(keys_ref, 0, True)
 
     order = [(other, lax.rem(y + k, YS)) for other in (1, 0) for k in (2, 1, 3, 0)]
     loads = []
@@ -283,13 +289,25 @@
 
         pltpu.make_async_copy(out_send.at[h, me], out_recv.at[h, me], back_recv_sem.at[h]).start()
         lax.fori_loop(1, CTX, reply, 0)
+        if h == 0:
+            keys_of.step_own(0)
+        else:
+            keys_of.step_near(0)
 
     for copy in gates_in:
         copy.wait()
     for h in range(2):
         pltpu.make_async_copy(out_recv.at[h], out_recv.at[h], back_recv_sem.at[h]).wait()
-
-    keys_of.scatter(keys_ref, True)
+        for s in range(4):
+            parts = [out_recv[h, line[s] * 8 + dl] for dl in range(8)]
+            filtered = nt(eye, jnp.concatenate(parts, axis=0)).astype(BF).astype(F32)
+            lanes = slice(h * 128, (h + 1) * 128)
+            cols = pl.ds(pl.multiple_of(line[s] * 256 + h * 128, 128), 128)
+            gated_ref[:, cols] = (
+                second_in[s, :, lanes].astype(F32)
+                * (filtered + skip[:, cols] * product[s, :, lanes].astype(F32))
+            ).astype(BF)
+
     far_pair = lax.min(z, ZS - 1 - z)
     q_x = lax.select(far_pair < 2, x, mirror)
     q_core = lax.rem(far_pair, 2)
@@ -310,13 +328,6 @@
 
     for j in range(4):
         start_either(*query_copies(j))
-
-    for s in range(4):
-        parts = [out_recv[h, line[s] * 8 + dl] for dl in range(8) for h in range(2)]
-        filtered = nt(eye, jnp.concatenate(parts, axis=0)).astype(BF).astype(F32)
-        gated_ref[:, cols_of[s]] = (
-            second_in[s].astype(F32) * (filtered + skip[:, cols_of[s]] * product[s].astype(F32))
-        ).astype(BF)
 
     gated = gated_ref[...]
     swaps = []
@@ -338,43 +349,35 @@
         return own_part[k] + sib_recv[k].astype(F32)
 
     right, left = lax.rem(y + 1, YS) * 2 + c, lax.rem(y + 3, YS) * 2 + c
+    depth = ROWS // PARTS
+    spans = [pl.ds(p * depth, depth) for p in range(PARTS)]
+
+    def hop(source, into, send_sems, recv_sems, h, p):
+        return pltpu.make_async_remote_copy(
+            src_ref=source.at[h, spans[p]], dst_ref=into.at[h, spans[p]],
+            send_sem=send_sems.at[h, p], recv_sem=recv_sems.at[h, p],
+            device_id={"tp": (right, left)[h]}, device_id_type=MESH,
+        )
+
     far = chip_sum(0).astype(BF)
-    hops = []
-    for h, to in ((0, right), (1, left)):
+    far_hops, near_hops = {}, {}
+    for h in range(2):
         y_send[h] = far[:, h * 256:(h + 1) * 256]
-        hops.append(pltpu.make_async_remote_copy(
-            src_ref=y_send.at[h], dst_ref=y_recv.at[h],
-            send_sem=y_send_sem.at[h], recv_sem=y_recv_sem.at[h],
-            device_id={"tp": to}, device_id_type=MESH,
-        ))
-        hops[-1].start()
+    for p in range(PARTS):
+        for h in range(2):
+            far_hops[h, p] = hop(y_send, y_recv, y_send_sem, y_recv_sem, h, p)
+            far_hops[h, p].start()
     for k in range(1, 4):
         own_part[k] = chip_sum(k)
-    for i in range(4):
-        keys_of.step_own(i)
-    for h, to in ((0, right), (1, left)):
-        hops[h].wait_recv()
-        cols = pl.ds(h * 256, 256)
-        own_part[1 + h, :, cols] += y_recv[h].astype(F32)
-        near_send[h] = own_part[1 + h].astype(BF)
-        hops.append(pltpu.make_async_remote_copy(
-            src_ref=near_send.at[h], dst_ref=near_recv.at[h],
-            send_sem=near_send_sem.at[h], recv_sem=near_recv_sem.at[h],
-            device_id={"tp": to}, device_id_type=MESH,
-        ))
-        hops[-1].start()
-    for i in range(4):
-        keys_of.step_near(i)
-    for h in range(2):
-        hops[2 + h].wait_recv()
-    mixed = (own_part[3] + near_recv[0].astype(F32) + near_recv[1].astype(F32)).astype(BF)
-    mine[...] = mixed
-    values_of.scatter(mine, True)
-    mixed_ref[...] = mixed
-    for i in range(4):
-        keys_of.step_far(i)
-    for i in range(4):
-        keys_of.finish(i)
+    keys_of.step_far(0)
+    for p in range(PARTS):
+        for h in range(2):
+            far_hops[h, p].wait_recv()
+            own_part[1 + h, spans[p], pl.ds(h * 256, 256)] += y_recv[h, spans[p]].astype(F32)
+            near_send[h, spans[p]] = own_part[1 + h, spans[p]].astype(BF)
+            near_hops[h, p] = hop(near_send, near_recv, near_send_sem, near_recv_sem, h, p)
+            near_hops[h, p].start()
+    keys_of.finish(0)
 
     scale = 1.0 / math.sqrt(HS) * math.log2(math.e)
     blocks, first_step = [], []
@@ -389,7 +392,8 @@
         steps_before = steps_before + lax.div(rank, 2) + 1
 
     def chunk(buf, step):
-        return buf[lax.div(step, 4), pl.ds(lax.rem(step, 4) * 2, 2)].reshape(KEYS, HS)
+        row, i = lax.div(step, 4), lax.rem(step, 4)
+        return jnp.concatenate([buf[row, 0, i], buf[row, 1, i]], axis=0)
 
     def fold(op, top, s):
         for at in range(0, KEYS, 128):
@@ -423,17 +427,26 @@
         totals[i] = jnp.broadcast_to(jnp.sum(total, axis=1, keepdims=True), (ROWS, 128))
 
     weigh(0)
+    for p in range(PARTS):
+        for h in range(2):
+            near_hops[h, p].wait_recv()
+        mixed = (
+            own_part[3, spans[p]] + near_recv[0, spans[p]].astype(F32) + near_recv[1, spans[p]].astype(F32)
+        ).astype(BF)
+        mine[spans[p]] = mixed
+        values_of.scatter(mine, p, True)
+        mixed_ref[spans[p]] = mixed
     weigh(1)
-    for i in range(4):
-        values_of.step_own(i)
+    values_of.step_own(0)
     weigh(2)
+    values_of.step_own(1)
+    values_of.step_near(0)
     weigh(3)
-    for i in range(4):
-        values_of.step_near(i)
-    for i in range(4):
-        values_of.step_far(i)
-    for i in range(4):
-        values_of.finish(i)
+    values_of.step_near(1)
+    values_of.step_far(0)
+    values_of.step_far(1)
+    for p in range(PARTS):
+        values_of.finish(p)
 
     def output_copies(i):
         row, zq, rank, last = blocks[i]
@@ -462,13 +475,18 @@
         pltpu.make_async_copy(some, some, send_sem.at[h]).wait()
         some = out_recv.at[h, pl.ds(0, CTX - 1)]
         pltpu.make_async_copy(some, some, back_send_sem.at[h]).wait()
-    keys_of.scatter(keys_ref, False)
-    values_of.scatter(mine, False)
+    keys_of.scatter(keys_ref, 0, False)
+    keys_of.drain(0)
+    for p in range(PARTS):
+        values_of.scatter(mine, p, False)
+        values_of.drain(p)
+        for h in range(2):
+            far_hops[h, p].wait_send()
+            near_hops[h, p].wait_send()
     for j in range(4):
         alone, local, away = query_copies(j)
         pl.when(jnp.logical_not(alone))(lambda away=away: away().wait_send())
         swaps[j].wait_send()
-        hops[j].wait_send()
     for j in range(4):
         pltpu.make_async_copy(o_recv.at[j], o_recv.at[j], o_recv_sem.at[j]).wait()
         attended_ref[:, j * HS:(j + 1) * HS] = o_recv[j]
@@ -490,15 +508,9 @@
     return [pl.BlockSpec(memory_space=pl.ANY)] * count
 
 
-def hand_over(a, b, a_out, b_out, sem):
-    copies = [
-        pltpu.make_async_copy(a, a_out, sem.at[0]),
-        pltpu.make_async_copy(b, b_out, sem.at[1]),
-    ]
-    for copy in copies:
-        copy.start()
-    for copy in copies:
-        copy.wait()
+def hand_over(a, b, a_out, b_out):
+    a_out[...] = a[...]
+    b_out[...] = b[...]
 
 
 def per_device(
@@ -509,7 +521,7 @@
     dma = lambda *shape: pltpu.SemaphoreType.DMA(shape)
     bf = lambda *shape: pltpu.VMEM(shape, BF)
     fl = lambda *shape: pltpu.VMEM(shape, F32)
-    sems = [dma(4), dma(4), dma(4), dma(4), dma(2, 4), dma(4), dma(4)]
+    sems = lambda p: [dma(p, 4), dma(p), dma(p), dma(p), dma(2, p), dma(XS, p), dma(2, p)]
     out = jax.ShapeDtypeStruct((ROWS, HEAD), BF)
     mixed, attended = pl.pallas_call(
         whole_kernel,
@@ -525,13 +537,13 @@
             bf(ROWS, 1024),
             bf(8, 1024, HEAD), fl(4, ROWS, HEAD), bf(4, ROWS, HEAD), bf(4, ROWS, HEAD),
             bf(2, ROWS, 256), bf(2, ROWS, 256), bf(2, ROWS, HEAD), bf(2, ROWS, HEAD), bf(ROWS, HEAD),
-            bf(XS, ZS, ROWS, HS), bf(XS, ZS, ROWS, HS), bf(4, ROWS, HS),
+            bf(XS, 2, ZS // 2, ROWS, HS), bf(XS, 2, ZS // 2, ROWS, HS), bf(4, ROWS, HS),
             fl(TOTAL // KEYS, ROWS, KEYS), bf(CHUNKS, ROWS, KEYS), fl(4, ROWS, 128),
             bf(4, ROWS, HS), bf(4, ROWS, HS),
             dma(4, 4), dma(6), dma(2), dma(2), dma(2), dma(2),
-            dma(8), dma(4), dma(4), dma(2), dma(2), dma(2), dma(2),
+            dma(8), dma(4), dma(4), dma(2, PARTS), dma(2, PARTS), dma(2, PARTS), dma(2, PARTS),
             dma(4), dma(4), dma(4), dma(4),
-        ] + sems + sems,
+        ] + sems(1) + sems(PARTS),
         compiler_params=pltpu.CompilerParams(
             collective_id=0, has_side_effects=True, vmem_limit_bytes=60 * 1024 * 1024
         ),
@@ -541,9 +553,8 @@
     return pl.pallas_call(
         hand_over,
         out_shape=(out, out),
-        in_specs=hbm(2),
-        out_specs=tuple(hbm(2)),
-        scratch_shapes=[dma(2)],
+        in_specs=vmem(2),
+        out_specs=tuple(vmem(2)),
         name="hand_over",
     )(mixed, attended)
 

time: 127 us -> 111 us (0.87)
  the two profiles are of different devices: /device:TPU:121 before, /device:TPU:64 now
where the time goes in v3:
time: 111 us
  Pallas kernels  110 us (99%)
    pallas_call x1, Pallas kernels, per_device(): pl.pallas_call(whole_kernel, out_shape=(out, out), in_specs=hbm(13), out_...  108 us

profile of v3, /device:TPU:64, one launch (start us, length us, event | category | flops | bytes accessed | tf_op | source)
XLA Modules:
  0.0 110.7 jit_solution(16756859381234860238)
XLA Ops:
  0.6 108.2 %whole.1 = (bf16[256,512]{1,0:T(8,128)(2,1)}, bf16[256,512]{1,0:T(8,128)(2,1)}) custom-call(bf16[256,1024]{1,0:T(8,128)(2,1)} %first_hbm.1, bf16[256,1024]{1,0:T(8,128)(2,1)} %second_hbm.1, bf16[256,1024]{1,0:T(8,128)(2,1)} %value_hbm.1, bf16[256,1024]{1,0:T(8,128)(2,1)} %taps_hbm.1, f32[1,1024]{1,0:T(1,128)} %bitcast.1, bf16[1024,4096]{1,0:T(8,128)(2,1)} %weight_ref.1, ...), custom_call_target="tpu_custom_call" | custom-call | tf_op jit(solution)/shard_map/whole/pallas_call | solution.py:526
  108.8 1.8 %hand_over.1 = (bf16[256,512]{1,0:T(8,128)(2,1)}, bf16[256,512]{1,0:T(8,128)(2,1)}) custom-call(bf16[256,512]{1,0:T(8,128)(2,1)} %get-tuple-element.4.a, bf16[256,512]{1,0:T(8,128)(2,1)} %get-tuple-element.5.b), custom_call_target="tpu_custom_call" | custom-call | tf_op jit(solution)/shard_map/hand_over/pallas_call | solution.py:553

commit v4 on v3

--- a/solution.py
+++ b/solution.py
@@ -145,8 +145,8 @@
     first_hbm, second_hbm, value_hbm, taps_hbm, skip_hbm, weight_ref, queries_ref, keys_ref,
     spread_hbm, mix_hbm, unmix_hbm, gather_hbm, turn_hbm, mixed_ref, attended_ref,
     first_in, value_in, taps_in, second_in, skip, spread_t, mix_t, unmix_t, gather_t, turn,
-    product, send, recv, out_send, out_recv, gated_ref,
-    weights, own_part, sib_send, sib_recv, y_send, y_recv, near_send, near_recv, mine,
+    product, send, recv, taps_spectrum, out_send, out_recv, gated_ref,
+    weights, partial, own_part, sib_send, sib_recv, y_send, y_recv, near_send, near_recv, mine,
     k_buf, v_buf, q_buf, scores, rounded, totals, o_send, o_recv,
     in_sem, table_sem, send_sem, recv_sem, back_send_sem, back_recv_sem,
     w_sem, sib_send_sem, sib_recv_sem, y_send_sem, y_recv_sem, near_send_sem, near_recv_sem,
@@ -163,15 +163,20 @@
     mirror = XS - 1 - x
     half = GROUP * CTX
 
-    line = [lax.rem(x + s, XS) for s in range(4)]
-    cols_of = [pl.ds(pl.multiple_of(at * 256, 256), 256) for at in line]
-    inputs = []
-    for s in range(4):
+    base = [lax.rem(lax.div(me, 16) + g, 2) * 16 for g in range(2)]
+    cols_of = [
+        [pl.ds(pl.multiple_of(h * 512 + base[g] * GROUP, 256), 256) for g in range(2)] for h in range(2)
+    ]
+    inputs = {}
+    for h in range(2):
         for k, (hbm, into) in enumerate(
             ((taps_hbm, taps_in), (first_hbm, first_in), (value_hbm, value_in))
         ):
-            inputs.append(pltpu.make_async_copy(hbm.at[:, cols_of[s]], into.at[s], in_sem.at[k, s]))
-            inputs[-1].start()
+            for g in range(2):
+                inputs[k, h, g] = pltpu.make_async_copy(
+                    hbm.at[:, cols_of[h][g]], into.at[h, g], in_sem.at[k, 2 * h + g]
+                )
+                inputs[k, h, g].start()
 
     barrier = pltpu.get_barrier_semaphore()
 
@@ -202,51 +207,47 @@
         tables_in.append(pltpu.make_async_copy(hbm, into, table_sem.at[k]))
         tables_in[-1].start()
     gates_in = []
-    for s in range(4):
-        gates_in.append(
-            pltpu.make_async_copy(second_hbm.at[:, cols_of[s]], second_in.at[s], in_sem.at[3, s])
-        )
-        gates_in[-1].start()
-
-    def post(h, s, k):
-        zt = lax.rem(z + k, ZS)
-        pltpu.make_async_remote_copy(
-            src_ref=send.at[h, s, zt], dst_ref=recv.at[h, me],
-            send_sem=send_sem.at[h], recv_sem=recv_sem.at[h],
-            device_id={"ctx": line[s] * ZS + zt}, device_id_type=MESH,
-        ).start()
-
-    def post_line(h, s):
+    for h in range(2):
+        for g in range(2):
+            gates_in.append(pltpu.make_async_copy(
+                second_hbm.at[:, cols_of[h][g]], second_in.at[h, g], in_sem.at[3, 2 * h + g]
+            ))
+            gates_in[-1].start()
+
+    def post_line(kind, h, g):
         def one(k, carry):
-            post(h, s, k)
+            o = lax.rem(me + k, 16)
+            pltpu.make_async_remote_copy(
+                src_ref=send.at[kind, h, g, o], dst_ref=recv.at[kind, h, me],
+                send_sem=send_sem.at[kind, h], recv_sem=recv_sem.at[kind, h],
+                device_id={"ctx": base[g] + o}, device_id_type=MESH,
+            ).start()
             return carry
 
-        if s == 0:
-            pltpu.make_async_copy(send.at[h, 0, z], recv.at[h, me], recv_sem.at[h]).start()
-        lax.fori_loop(1 if s == 0 else 0, ZS, one, 0)
-
-    def same(rows):
-        down = lax.broadcasted_iota(jnp.int32, (rows, rows), 0)
-        across = lax.broadcasted_iota(jnp.int32, (rows, rows), 1)
-        return jnp.where(down == across, 1.0, 0.0).astype(BF)
-
-    eye = same(ROWS)
-    for s in range(4):
-        for copy in inputs[3 * s:3 * s + 3]:
-            copy.wait()
-        prod = (first_in[s].astype(F32) * value_in[s].astype(F32)).astype(BF)
-        product[s] = prod
-        for kind, block in ((0, prod), (1, taps_in[s])):
-            turned = nt(eye, block).astype(BF)
-            for dl in range(8):
-                for h in range(2):
-                    at = h * 128 + dl * GROUP
-                    send[h, s, dl, kind] = turned[at:at + GROUP]
-        if s == 0:
-            pl.semaphore_wait(barrier, CTX - 1 + 2 * ZS + 2)
-        post_line(0, s)
-    for s in range(4):
-        post_line(1, s)
+        if g == 0:
+            pltpu.make_async_copy(
+                send.at[kind, h, 0, lax.rem(me, 16)], recv.at[kind, h, me], recv_sem.at[kind, h]
+            ).start()
+        lax.fori_loop(1 if g == 0 else 0, 16, one, 0)
+
+    down = lax.broadcasted_iota(jnp.int32, (ROWS, ROWS), 0)
+    across = lax.broadcasted_iota(jnp.int32, (ROWS, ROWS), 1)
+    eye = jnp.where(down == across, 1.0, 0.0).astype(BF)
+    for h in range(2):
+        for kind in (1, 0):
+            for g in range(2):
+                if kind == 1:
+                    inputs[0, h, g].wait()
+                    block = taps_in[h, g]
+                else:
+                    inputs[1, h, g].wait()
+                    inputs[2, h, g].wait()
+                    block = (first_in[h, g].astype(F32) * value_in[h, g].astype(F32)).astype(BF)
+                    product[h, g] = block
+                send[kind, h, g] = nt(eye, block).astype(BF).reshape(16, GROUP, ROWS)
+                if (h, kind, g) == (0, 1, 0):
+                    pl.semaphore_wait(barrier, CTX - 1 + 2 * ZS + 2)
+                post_line(kind, h, g)
     keys_of.scatter(keys_ref, 0, True)
 
     order = [(other, lax.rem(y + k, YS)) for other in (1, 0) for k in (2, 1, 3, 0)]
@@ -261,12 +262,14 @@
         copy.wait()
 
     for h in range(2):
-        pltpu.make_async_copy(recv.at[h], recv.at[h], recv_sem.at[h]).wait()
         tr, ti = turn[:CTX], turn[CTX:]
-        xs = recv[h, :, 0].reshape(half, ROWS)
-        ws = recv[h, :, 1].reshape(half, ROWS)
-        d = spectrum(xs, spread_t[...], mix_t[...], tr, ti)
-        e = spectrum(ws, spread_t[...], mix_t[...], tr, ti)
+        pltpu.make_async_copy(recv.at[1, h], recv.at[1, h], recv_sem.at[1, h]).wait()
+        taps_spectrum[...] = spectrum(
+            recv[1, h].reshape(half, ROWS), spread_t[...], mix_t[...], tr, ti
+        )
+        pltpu.make_async_copy(recv.at[0, h], recv.at[0, h], recv_sem.at[0, h]).wait()
+        d = spectrum(recv[0, h].reshape(half, ROWS), spread_t[...], mix_t[...], tr, ti)
+        e = taps_spectrum[...]
         d_re, d_im, e_re, e_im = d[:, :ROWS], d[:, ROWS:], e[:, :ROWS], e[:, ROWS:]
         y_re = (d_re * e_re - d_im * e_im).astype(BF)
         y_im = (d_re * e_im + d_im * e_re).astype(BF)
@@ -296,22 +299,32 @@
 
     for copy in gates_in:
         copy.wait()
-    for h in range(2):
+
+    def gate(h):
         pltpu.make_async_copy(out_recv.at[h], out_recv.at[h], back_recv_sem.at[h]).wait()
-        for s in range(4):
-            parts = [out_recv[h, line[s] * 8 + dl] for dl in range(8)]
-            filtered = nt(eye, jnp.concatenate(parts, axis=0)).astype(BF).astype(F32)
-            lanes = slice(h * 128, (h + 1) * 128)
-            cols = pl.ds(pl.multiple_of(line[s] * 256 + h * 128, 128), 128)
-            gated_ref[:, cols] = (
-                second_in[s, :, lanes].astype(F32)
-                * (filtered + skip[:, cols] * product[s, :, lanes].astype(F32))
+        for g in range(2):
+            block = out_recv[h, pl.ds(base[g], 16)].reshape(ROWS, ROWS)
+            filtered = nt(eye, block).astype(BF).astype(F32)
+            gated_ref[:, cols_of[h][g]] = (
+                second_in[h, g].astype(F32)
+                * (filtered + skip[:, cols_of[h][g]] * product[h, g].astype(F32))
             ).astype(BF)
+
+    gate(0)
+    low = gated_ref[:, :512]
+    for k in range(8):
+        loads[k].wait()
+        partial[k] = nn(low, weights[k, :512])
+    gate(1)
+    high = gated_ref[:, 512:]
+
+    def projected(k):
+        return partial[k] + nn(high, weights[k, 512:])
 
     far_pair = lax.min(z, ZS - 1 - z)
     q_x = lax.select(far_pair < 2, x, mirror)
     q_core = lax.rem(far_pair, 2)
-    q_slot = lax.div(far_pair, 2) * 2 + lax.div(z, 4)
+    q_slot = lax.div(x, 2) * 2 + lax.div(z, 4)
 
     def query_copies(j):
         to = 4 * c + j
@@ -329,24 +342,20 @@
     for j in range(4):
         start_either(*query_copies(j))
 
-    gated = gated_ref[...]
     swaps = []
     for k in range(4):
-        loads[k].wait()
-        sib_send[k] = nn(gated, weights[k]).astype(BF)
+        sib_send[k] = projected(k).astype(BF)
         swaps.append(pltpu.make_async_remote_copy(
             src_ref=sib_send.at[k], dst_ref=sib_recv.at[k],
             send_sem=sib_send_sem.at[k], recv_sem=sib_recv_sem.at[k],
             device_id={"tp": y * 2 + 1 - c}, device_id_type=MESH,
         ))
         swaps[-1].start()
-    for k in range(4):
-        loads[4 + k].wait()
-        own_part[k] = nn(gated, weights[4 + k])
 
     def chip_sum(k):
+        own = projected(4 + k)
         swaps[k].wait_recv()
-        return own_part[k] + sib_recv[k].astype(F32)
+        return own + sib_recv[k].astype(F32)
 
     right, left = lax.rem(y + 1, YS) * 2 + c, lax.rem(y + 3, YS) * 2 + c
     depth = ROWS // PARTS
@@ -383,8 +392,8 @@
     blocks, first_step = [], []
     steps_before = 0
     for i in range(4):
-        row = x if i < 2 else mirror
-        pair = c + 2 * (i // 2)
+        row = lax.min(x, mirror) if i < 2 else lax.max(x, mirror)
+        pair = lax.select(row == x, c, c + 2)
         zq = pair if i % 2 == 0 else ZS - 1 - pair
         rank = row * ZS + zq
         blocks.append((row, zq, rank, lax.div(rank, 2)))
@@ -400,7 +409,7 @@
             top = op(top, s[:, at:at + 128])
         return top
 
-    def weigh(i):
+    def score_all(i):
         row, zq, rank, last = blocks[i]
         pltpu.make_async_copy(q_buf.at[i], q_buf.at[i], q_recv_sem.at[i]).wait()
         query = q_buf[i]
@@ -417,6 +426,11 @@
         s = jnp.where(key_pos <= query_pos, s, NEG)
         scores[last] = s
         top = jnp.max(fold(jnp.maximum, top, s), axis=1, keepdims=True)
+        totals[i] = jnp.broadcast_to(top, (ROWS, 128))
+
+    def weigh_all(i):
+        row, zq, rank, last = blocks[i]
+        top = totals[i, :, :1]
 
         def weight(step, total):
             w = jnp.exp2((scores[step] - top) * scale)
@@ -426,8 +440,7 @@
         total = lax.fori_loop(0, last + 1, weight, jnp.zeros((ROWS, 128), F32))
         totals[i] = jnp.broadcast_to(jnp.sum(total, axis=1, keepdims=True), (ROWS, 128))
 
-    weigh(0)
-    for p in range(PARTS):
+    def values_out(p):
         for h in range(2):
             near_hops[h, p].wait_recv()
         mixed = (
@@ -436,12 +449,19 @@
         mine[spans[p]] = mixed
         values_of.scatter(mine, p, True)
         mixed_ref[spans[p]] = mixed
-    weigh(1)
+
+    for i in range(2):
+        score_all(i)
+        weigh_all(i)
+    values_out(0)
+    score_all(2)
+    values_out(1)
+    weigh_all(2)
     values_of.step_own(0)
-    weigh(2)
+    score_all(3)
     values_of.step_own(1)
+    weigh_all(3)
     values_of.step_near(0)
-    weigh(3)
     values_of.step_near(1)
     values_of.step_far(0)
     values_of.step_far(1)
@@ -471,8 +491,9 @@
         start_either(*output_copies(i))
 
     for h in range(2):
-        some = recv.at[h, pl.ds(0, CTX - 1)]
-        pltpu.make_async_copy(some, some, send_sem.at[h]).wait()
+        for kind in range(2):
+            some = recv.at[kind, h, pl.ds(0, CTX - 1)]
+            pltpu.make_async_copy(some, some, send_sem.at[kind, h]).wait()
         some = out_recv.at[h, pl.ds(0, CTX - 1)]
         pltpu.make_async_copy(some, some, back_send_sem.at[h]).wait()
     keys_of.scatter(keys_ref, 0, False)
@@ -529,18 +550,18 @@
         in_specs=hbm(13),
         out_specs=tuple(vmem(2)),
         scratch_shapes=[
-            bf(4, ROWS, 256), bf(4, ROWS, 256), bf(4, ROWS, 256), bf(4, ROWS, 256),
+            bf(2, 2, ROWS, 256), bf(2, 2, ROWS, 256), bf(2, 2, ROWS, 256), bf(2, 2, ROWS, 256),
             fl(1, 1024), bf(1024, 512), bf(512, 512), bf(512, 512), bf(512, 1024), fl(2 * CTX, ROWS),
-            bf(4, ROWS, 256),
-            bf(2, 4, 8, 2, GROUP, ROWS), bf(2, CTX, 2, GROUP, ROWS),
+            bf(2, 2, ROWS, 256),
+            bf(2, 2, 2, 16, GROUP, ROWS), bf(2, 2, CTX, GROUP, ROWS), fl(512, 512),
             bf(2, CTX, GROUP, ROWS), bf(2, CTX, GROUP, ROWS),
             bf(ROWS, 1024),
-            bf(8, 1024, HEAD), fl(4, ROWS, HEAD), bf(4, ROWS, HEAD), bf(4, ROWS, HEAD),
+            bf(8, 1024, HEAD), fl(8, ROWS, HEAD), fl(4, ROWS, HEAD), bf(4, ROWS, HEAD), bf(4, ROWS, HEAD),
             bf(2, ROWS, 256), bf(2, ROWS, 256), bf(2, ROWS, HEAD), bf(2, ROWS, HEAD), bf(ROWS, HEAD),
             bf(XS, 2, ZS // 2, ROWS, HS), bf(XS, 2, ZS // 2, ROWS, HS), bf(4, ROWS, HS),
             fl(TOTAL // KEYS, ROWS, KEYS), bf(CHUNKS, ROWS, KEYS), fl(4, ROWS, 128),
             bf(4, ROWS, HS), bf(4, ROWS, HS),
-            dma(4, 4), dma(6), dma(2), dma(2), dma(2), dma(2),
+            dma(4, 4), dma(6), dma(2, 2), dma(2, 2), dma(2), dma(2),
             dma(8), dma(4), dma(4), dma(2, PARTS), dma(2, PARTS), dma(2, PARTS), dma(2, PARTS),
             dma(4), dma(4), dma(4), dma(4),
         ] + sems(1) + sems(PARTS),

time: 111 us -> 106 us (0.955)
  the two profiles are of different devices: /device:TPU:64 before, /device:TPU:6 now
where the time goes in v4:
time: 106 us; the launch traced here: 105 us
  Pallas kernels  104 us (98%)
    pallas_call x1, Pallas kernels, per_device(): pl.pallas_call(whole_kernel, out_shape=(out, out), in_specs=hbm(13), out_...  103 us

profile of v4, /device:TPU:6, one launch (start us, length us, event | category | flops | bytes accessed | tf_op | source)
XLA Modules:
  0.0 105.0 jit_solution(3637729377014334548)
XLA Ops:
  0.6 102.5 %whole.1 = (bf16[256,512]{1,0:T(8,128)(2,1)}, bf16[256,512]{1,0:T(8,128)(2,1)}) custom-call(bf16[256,1024]{1,0:T(8,128)(2,1)} %first_hbm.1, bf16[256,1024]{1,0:T(8,128)(2,1)} %second_hbm.1, bf16[256,1024]{1,0:T(8,128)(2,1)} %value_hbm.1, bf16[256,1024]{1,0:T(8,128)(2,1)} %taps_hbm.1, f32[1,1024]{1,0:T(1,128)} %bitcast.1, bf16[1024,4096]{1,0:T(8,128)(2,1)} %weight_ref.1, ...), custom_call_target="tpu_custom_call" | custom-call | tf_op jit(solution)/shard_map/whole/pallas_call | solution.py:547
  103.2 1.8 %hand_over.1 = (bf16[256,512]{1,0:T(8,128)(2,1)}, bf16[256,512]{1,0:T(8,128)(2,1)}) custom-call(bf16[256,512]{1,0:T(8,128)(2,1)} %get-tuple-element.4.a, bf16[256,512]{1,0:T(8,128)(2,1)} %get-tuple-element.5.b), custom_call_target="tpu_custom_call" | custom-call | tf_op jit(solution)/shard_map/hand_over/pallas_call | solution.py:574

commit v5 on v4

--- a/solution.py
+++ b/solution.py
@@ -59,7 +59,7 @@
 
 XS, ZS, YS = 4, 8, 4
 HEAD = 512
-KEYS = 512
+KEYS = 1024
 NEG = -1e30
 
 
@@ -138,7 +138,7 @@
 
 
 PARTS = 2
-CHUNKS = 36
+CHUNKS = 20
 
 
 def whole_kernel(
@@ -396,49 +396,53 @@
         pair = lax.select(row == x, c, c + 2)
         zq = pair if i % 2 == 0 else ZS - 1 - pair
         rank = row * ZS + zq
-        blocks.append((row, zq, rank, lax.div(rank, 2)))
+        blocks.append((row, zq, rank, lax.div(rank, 4)))
         first_step.append(steps_before)
-        steps_before = steps_before + lax.div(rank, 2) + 1
-
-    def chunk(buf, step):
-        row, i = lax.div(step, 4), lax.rem(step, 4)
-        return jnp.concatenate([buf[row, 0, i], buf[row, 1, i]], axis=0)
-
-    def fold(op, top, s):
-        for at in range(0, KEYS, 128):
-            top = op(top, s[:, at:at + 128])
-        return top
+        steps_before = steps_before + lax.div(rank, 4) + 1
+
+    def key_block(buf, step, b):
+        return buf[lax.div(step, 2), b % 2, lax.rem(step, 2) * 2 + b // 2]
 
     def score_all(i):
         row, zq, rank, last = blocks[i]
         pltpu.make_async_copy(q_buf.at[i], q_buf.at[i], q_recv_sem.at[i]).wait()
         query = q_buf[i]
 
-        def score(step, top):
-            s = nt(query, chunk(k_buf, step))
-            scores[step] = s
-            return fold(jnp.maximum, top, s)
+        def score(step, top, masked=False):
+            for b in range(KEYS // ROWS):
+                s = nt(query, key_block(k_buf, step, b))
+                if masked:
+                    key_pos = across + step * KEYS + b * ROWS
+                    s = jnp.where(key_pos <= down + rank * ROWS, s, NEG)
+                scores[step, b] = s
+                top = jnp.maximum(top, jnp.maximum(s[:, :128], s[:, 128:]))
+            return top
 
         top = lax.fori_loop(0, last, score, jnp.full((ROWS, 128), NEG, F32))
-        s = nt(query, chunk(k_buf, last))
-        key_pos = lax.broadcasted_iota(jnp.int32, (ROWS, KEYS), 1) + last * KEYS
-        query_pos = lax.broadcasted_iota(jnp.int32, (ROWS, KEYS), 0) + rank * ROWS
-        s = jnp.where(key_pos <= query_pos, s, NEG)
-        scores[last] = s
-        top = jnp.max(fold(jnp.maximum, top, s), axis=1, keepdims=True)
+        top = jnp.max(score(last, top, True), axis=1, keepdims=True)
         totals[i] = jnp.broadcast_to(top, (ROWS, 128))
 
     def weigh_all(i):
         row, zq, rank, last = blocks[i]
-        top = totals[i, :, :1]
-
-        def weight(step, total):
-            w = jnp.exp2((scores[step] - top) * scale)
-            rounded[first_step[i] + step] = w.astype(BF)
-            return fold(jnp.add, total, w)
-
-        total = lax.fori_loop(0, last + 1, weight, jnp.zeros((ROWS, 128), F32))
-        totals[i] = jnp.broadcast_to(jnp.sum(total, axis=1, keepdims=True), (ROWS, 128))
+        totals_i = []
+        for r in range(2):
+            rows = slice(r * 128, (r + 1) * 128)
+            top = totals[i, rows]
+
+            def weight(step, total):
+                for b in range(KEYS // ROWS):
+                    for l in range(2):
+                        w = jnp.exp2((scores[step, b, rows, l * 128:(l + 1) * 128] - top) * scale)
+                        rounded[first_step[i] + step, rows, b * ROWS + l * 128:b * ROWS + (l + 1) * 128] = (
+                            w.astype(BF)
+                        )
+                        total = total + w
+                return total
+
+            totals_i.append(lax.fori_loop(0, last + 1, weight, jnp.zeros((128, 128), F32)))
+        for r in range(2):
+            total = jnp.sum(totals_i[r], axis=1, keepdims=True)
+            totals[i, r * 128:(r + 1) * 128] = jnp.broadcast_to(total, (128, 128))
 
     def values_out(p):
         for h in range(2):
@@ -484,7 +488,8 @@
         row, zq, rank, last = blocks[i]
 
         def value(step, acc, i=i):
-            return acc + nn(rounded[first_step[i] + step], chunk(v_buf, step))
+            part = jnp.concatenate([key_block(v_buf, step, b) for b in range(KEYS // ROWS)], axis=0)
+            return acc + nn(rounded[first_step[i] + step], part)
 
         acc = lax.fori_loop(0, last + 1, value, jnp.zeros((ROWS, HS), F32))
         o_send[i] = (acc / totals[i]).astype(BF)
@@ -559,7 +564,7 @@
             bf(8, 1024, HEAD), fl(8, ROWS, HEAD), fl(4, ROWS, HEAD), bf(4, ROWS, HEAD), bf(4, ROWS, HEAD),
             bf(2, ROWS, 256), bf(2, ROWS, 256), bf(2, ROWS, HEAD), bf(2, ROWS, HEAD), bf(ROWS, HEAD),
             bf(XS, 2, ZS // 2, ROWS, HS), bf(XS, 2, ZS // 2, ROWS, HS), bf(4, ROWS, HS),
-            fl(TOTAL // KEYS, ROWS, KEYS), bf(CHUNKS, ROWS, KEYS), fl(4, ROWS, 128),
+            fl(TOTAL // KEYS, KEYS // ROWS, ROWS, ROWS), bf(CHUNKS, ROWS, KEYS), fl(4, ROWS, 128),
             bf(4, ROWS, HS), bf(4, ROWS, HS),
             dma(4, 4), dma(6), dma(2, 2), dma(2, 2), dma(2), dma(2),
             dma(8), dma(4), dma(4), dma(2, PARTS), dma(2, PARTS), dma(2, PARTS), dma(2, PARTS),

time: 106 us -> 104 us (0.981)
    pallas_call x1, Pallas kernels: 103 us -> 101 us  [per_device(): pl.pallas_call(whole_kernel, out_shape=(out, out), in_specs=hbm(13), out_...]
where the time goes in v5:
time: 104 us
  Pallas kernels  103 us (99%)
    pallas_call x1, Pallas kernels, per_device(): pl.pallas_call(whole_kernel, out_shape=(out, out), in_specs=hbm(13), out_...  101 us

profile of v5, /device:TPU:6, one launch (start us, length us, event | category | flops | bytes accessed | tf_op | source)
XLA Modules:
  0.0 103.5 jit_solution(15870163688663879848)
XLA Ops:
  0.6 101.0 %whole.1 = (bf16[256,512]{1,0:T(8,128)(2,1)}, bf16[256,512]{1,0:T(8,128)(2,1)}) custom-call(bf16[256,1024]{1,0:T(8,128)(2,1)} %first_hbm.1, bf16[256,1024]{1,0:T(8,128)(2,1)} %second_hbm.1, bf16[256,1024]{1,0:T(8,128)(2,1)} %value_hbm.1, bf16[256,1024]{1,0:T(8,128)(2,1)} %taps_hbm.1, f32[1,1024]{1,0:T(1,128)} %bitcast.1, bf16[1024,4096]{1,0:T(8,128)(2,1)} %weight_ref.1, ...), custom_call_target="tpu_custom_call" | custom-call | tf_op jit(solution)/shard_map/whole/pallas_call | solution.py:552
  101.7 1.8 %hand_over.1 = (bf16[256,512]{1,0:T(8,128)(2,1)}, bf16[256,512]{1,0:T(8,128)(2,1)}) custom-call(bf16[256,512]{1,0:T(8,128)(2,1)} %get-tuple-element.4.a, bf16[256,512]{1,0:T(8,128)(2,1)} %get-tuple-element.5.b), custom_call_target="tpu_custom_call" | custom-call | tf_op jit(solution)/shard_map/hand_over/pallas_call | solution.py:579

commit v6 on v5

--- a/solution.py
+++ b/solution.py
@@ -128,8 +128,8 @@
             self.arrived(half, self.far.at[h, p])
             self.push(half, p, self.x, 1 - self.c, self.sib.at[self.x2, p])
 
-    def finish(self, p):
-        for x in range(XS):
+    def finish(self, x, parts):
+        for p in range(parts):
             self.arrived(self.buf.at[x, 1 - self.c, :, self.span(p)], self.sib.at[x, p])
 
     def drain(self, p):
@@ -147,7 +147,7 @@
     first_in, value_in, taps_in, second_in, skip, spread_t, mix_t, unmix_t, gather_t, turn,
     product, send, recv, taps_spectrum, out_send, out_recv, gated_ref,
     weights, partial, own_part, sib_send, sib_recv, y_send, y_recv, near_send, near_recv, mine,
-    k_buf, v_buf, q_buf, scores, rounded, totals, o_send, o_recv,
+    k_buf, v_buf, q_buf, scores, rounded, totals, attended_sum, o_send, o_recv,
     in_sem, table_sem, send_sem, recv_sem, back_send_sem, back_recv_sem,
     w_sem, sib_send_sem, sib_recv_sem, y_send_sem, y_recv_sem, near_send_sem, near_recv_sem,
     q_send_sem, q_recv_sem, o_send_sem, o_recv_sem,
@@ -386,7 +386,8 @@
             near_send[h, spans[p]] = own_part[1 + h, spans[p]].astype(BF)
             near_hops[h, p] = hop(near_send, near_recv, near_send_sem, near_recv_sem, h, p)
             near_hops[h, p].start()
-    keys_of.finish(0)
+    for row in range(XS):
+        keys_of.finish(row, 1)
 
     scale = 1.0 / math.sqrt(HS) * math.log2(math.e)
     blocks, first_step = [], []
@@ -422,27 +423,27 @@
         top = jnp.max(score(last, top, True), axis=1, keepdims=True)
         totals[i] = jnp.broadcast_to(top, (ROWS, 128))
 
+    def weigh_half(i, r):
+        row, zq, rank, last = blocks[i]
+        rows = slice(r * 128, (r + 1) * 128)
+        top = totals[i, rows]
+
+        def weight(step, total):
+            for b in range(KEYS // ROWS):
+                for l in range(2):
+                    w = jnp.exp2((scores[step, b, rows, l * 128:(l + 1) * 128] - top) * scale)
+                    rounded[first_step[i] + step, rows, b * ROWS + l * 128:b * ROWS + (l + 1) * 128] = (
+                        w.astype(BF)
+                    )
+                    total = total + w
+            return total
+
+        total = lax.fori_loop(0, last + 1, weight, jnp.zeros((128, 128), F32))
+        totals[i, rows] = jnp.broadcast_to(jnp.sum(total, axis=1, keepdims=True), (128, 128))
+
     def weigh_all(i):
-        row, zq, rank, last = blocks[i]
-        totals_i = []
         for r in range(2):
-            rows = slice(r * 128, (r + 1) * 128)
-            top = totals[i, rows]
-
-            def weight(step, total):
-                for b in range(KEYS // ROWS):
-                    for l in range(2):
-                        w = jnp.exp2((scores[step, b, rows, l * 128:(l + 1) * 128] - top) * scale)
-                        rounded[first_step[i] + step, rows, b * ROWS + l * 128:b * ROWS + (l + 1) * 128] = (
-                            w.astype(BF)
-                        )
-                        total = total + w
-                return total
-
-            totals_i.append(lax.fori_loop(0, last + 1, weight, jnp.zeros((128, 128), F32)))
-        for r in range(2):
-            total = jnp.sum(totals_i[r], axis=1, keepdims=True)
-            totals[i, r * 128:(r + 1) * 128] = jnp.broadcast_to(total, (128, 128))
+            weigh_half(i, r)
 
     def values_out(p):
         for h in range(2):
@@ -464,13 +465,10 @@
     values_of.step_own(0)
     score_all(3)
     values_of.step_own(1)
-    weigh_all(3)
+    weigh_half(3, 0)
     values_of.step_near(0)
+    weigh_half(3, 1)
     values_of.step_near(1)
-    values_of.step_far(0)
-    values_of.step_far(1)
-    for p in range(PARTS):
-        values_of.finish(p)
 
     def output_copies(i):
         row, zq, rank, last = blocks[i]
@@ -484,16 +482,42 @@
         )
         return alone, local, away
 
-    for i in range(4):
-        row, zq, rank, last = blocks[i]
-
-        def value(step, acc, i=i):
+    def attend_row(row, i, first=False):
+        last = blocks[i][3]
+
+        def value(step, acc):
             part = jnp.concatenate([key_block(v_buf, step, b) for b in range(KEYS // ROWS)], axis=0)
             return acc + nn(rounded[first_step[i] + step], part)
 
-        acc = lax.fori_loop(0, last + 1, value, jnp.zeros((ROWS, HS), F32))
-        o_send[i] = (acc / totals[i]).astype(BF)
+        start = jnp.zeros((ROWS, HS), F32) if first else attended_sum[i]
+        attended_sum[i] = lax.fori_loop(2 * row, lax.min(2 * row + 2, last + 1), value, start)
+
+    def output(i):
+        o_send[i] = (attended_sum[i] / totals[i]).astype(BF)
         start_either(*output_copies(i))
+
+    def output_low():
+        output(0)
+        output(1)
+
+    xl, xr, x2 = values_of.xl, values_of.xr, values_of.x2
+    values_of.finish(x, PARTS)
+    for i in range(4):
+        attend_row(x, i, True)
+    values_of.step_far(0)
+    values_of.step_far(1)
+    for row in (xl, xr):
+        values_of.finish(row, PARTS)
+        for i in range(4):
+            attend_row(row, i)
+    pl.when(x != 2)(output_low)
+    values_of.finish(x2, PARTS)
+    for i in (2, 3):
+        attend_row(x2, i)
+        output(i)
+    for i in (0, 1):
+        attend_row(x2, i)
+    pl.when(x == 2)(output_low)
 
     for h in range(2):
         for kind in range(2):
@@ -564,7 +588,7 @@
             bf(8, 1024, HEAD), fl(8, ROWS, HEAD), fl(4, ROWS, HEAD), bf(4, ROWS, HEAD), bf(4, ROWS, HEAD),
             bf(2, ROWS, 256), bf(2, ROWS, 256), bf(2, ROWS, HEAD), bf(2, ROWS, HEAD), bf(ROWS, HEAD),
             bf(XS, 2, ZS // 2, ROWS, HS), bf(XS, 2, ZS // 2, ROWS, HS), bf(4, ROWS, HS),
-            fl(TOTAL // KEYS, KEYS // ROWS, ROWS, ROWS), bf(CHUNKS, ROWS, KEYS), fl(4, ROWS, 128),
+            fl(TOTAL // KEYS, KEYS // ROWS, ROWS, ROWS), bf(CHUNKS, ROWS, KEYS), fl(4, ROWS, 128), fl(4, ROWS, HS),
             bf(4, ROWS, HS), bf(4, ROWS, HS),
             dma(4, 4), dma(6), dma(2, 2), dma(2, 2), dma(2), dma(2),
             dma(8), dma(4), dma(4), dma(2, PARTS), dma(2, PARTS), dma(2, PARTS), dma(2, PARTS),

time: 104 us -> 103 us (level)
  no operation moved by 1% of the time
where the time goes in v6:
time: 103 us
  Pallas kernels  103 us (100%)
    pallas_call x1, Pallas kernels, per_device(): pl.pallas_call(whole_kernel, out_shape=(out, out), in_specs=hbm(13), out_...  101 us

profile of v6, /device:TPU:6, one launch (start us, length us, event | category | flops | bytes accessed | tf_op | source)
XLA Modules:
  0.0 103.2 jit_solution(11868125318659208780)
XLA Ops:
  0.6 100.7 %whole.1 = (bf16[256,512]{1,0:T(8,128)(2,1)}, bf16[256,512]{1,0:T(8,128)(2,1)}) custom-call(bf16[256,1024]{1,0:T(8,128)(2,1)} %first_hbm.1, bf16[256,1024]{1,0:T(8,128)(2,1)} %second_hbm.1, bf16[256,1024]{1,0:T(8,128)(2,1)} %value_hbm.1, bf16[256,1024]{1,0:T(8,128)(2,1)} %taps_hbm.1, f32[1,1024]{1,0:T(1,128)} %bitcast.1, bf16[1024,4096]{1,0:T(8,128)(2,1)} %weight_ref.1, ...), custom_call_target="tpu_custom_call" | custom-call | tf_op jit(solution)/shard_map/whole/pallas_call | solution.py:576
  101.3 1.8 %hand_over.1 = (bf16[256,512]{1,0:T(8,128)(2,1)}, bf16[256,512]{1,0:T(8,128)(2,1)}) custom-call(bf16[256,512]{1,0:T(8,128)(2,1)} %get-tuple-element.4.a, bf16[256,512]{1,0:T(8,128)(2,1)} %get-tuple-element.5.b), custom_call_target="tpu_custom_call" | custom-call | tf_op jit(solution)/shard_map/hand_over/pallas_call | solution.py:603

commit v7 on v6

--- a/solution.py
+++ b/solution.py
@@ -34,17 +34,35 @@
     rows = np.exp(-2j * np.pi * np.outer(q + 0.25, r) / CTX)
     turn = np.exp(-2j * np.pi * np.outer(q + 0.25, a) / TOTAL)
     cols = np.exp(-2j * np.pi * np.outer(a, a) / ROWS)
-    eye = np.eye(GROUP)
-    spread = lambda m: np.einsum("qr,cd->cqrd", m, eye).reshape(GROUP * CTX, CTX * GROUP)
-    first = np.concatenate([spread(rows.real), spread(rows.imag)], axis=0)
-    back = np.conj(rows).T
-    gather = lambda m: np.einsum("rq,cd->rcdq", m, eye).reshape(CTX * GROUP, GROUP * CTX)
-    last = np.concatenate([gather(back.real), -gather(back.imag)], axis=1)
-    mix = np.block([[cols.real, cols.imag], [-cols.imag, cols.real]])
-    unmix = np.block([[cols.real, -cols.imag], [cols.imag, cols.real]]) / TOTAL
+    parts = lambda m: np.concatenate([m.real, m.imag], axis=0)
     cast = lambda m: np.asarray(m, np.float32).astype(jnp.bfloat16)
-    return (cast(first), cast(mix), cast(unmix), cast(last),
-            np.asarray(turn.real, np.float32), np.asarray(turn.imag, np.float32))
+    return (cast(np.repeat(parts(rows), GROUP, axis=1)), cast(parts(cols)),
+            np.asarray(parts(turn), np.float32))
+
+
+def build_tables(rows_ref, cols_ref, eye, spread_t, mix_t, unmix_t, gather_t):
+    column = lax.rem(lax.broadcasted_iota(jnp.int32, (CTX, CTX * GROUP), 1), GROUP)
+    half = GROUP * CTX
+    for part in range(2):
+        values = rows_ref[part * CTX:(part + 1) * CTX].astype(F32)
+        for c in range(GROUP):
+            at = part * half + c * CTX
+            spread_t[at:at + CTX] = jnp.where(column == c, values, 0.0).astype(BF)
+    for i in range(2):
+        for j in range(4):
+            a, b = slice(i * 256, (i + 1) * 256), slice(j * 256, (j + 1) * 256)
+            gather_t[a, b] = nt(eye, spread_t[b, a]).astype(BF)
+    re, im = cols_ref[:ROWS].astype(F32), cols_ref[ROWS:].astype(F32)
+    top, low = slice(0, ROWS), slice(ROWS, 2 * ROWS)
+    mix_t[top, top] = re.astype(BF)
+    mix_t[low, low] = re.astype(BF)
+    mix_t[top, low] = im.astype(BF)
+    mix_t[low, top] = (-im).astype(BF)
+    re, im = re * (1.0 / TOTAL), im * (1.0 / TOTAL)
+    unmix_t[top, top] = re.astype(BF)
+    unmix_t[low, low] = re.astype(BF)
+    unmix_t[top, low] = (-im).astype(BF)
+    unmix_t[low, top] = im.astype(BF)
 
 
 def spectrum(x, first, mix, turn_re, turn_im):
@@ -143,12 +161,12 @@
 
 def whole_kernel(
     first_hbm, second_hbm, value_hbm, taps_hbm, skip_hbm, weight_ref, queries_ref, keys_ref,
-    spread_hbm, mix_hbm, unmix_hbm, gather_hbm, turn_hbm, mixed_ref, attended_ref,
-    first_in, value_in, taps_in, second_in, skip, spread_t, mix_t, unmix_t, gather_t, turn,
-    product, send, recv, taps_spectrum, out_send, out_recv, gated_ref,
+    rows_hbm, cols_hbm, turn_hbm, mixed_ref, attended_ref,
+    first_in, value_in, taps_in, second_in, skip, rows_in, cols_in, turn, spread_t, mix_t, unmix_t, gather_t,
+    product, send, recv, taps_send, taps_recv, taps_spectrum, out_send, out_recv, gated_ref,
     weights, partial, own_part, sib_send, sib_recv, y_send, y_recv, near_send, near_recv, mine,
     k_buf, v_buf, q_buf, scores, rounded, totals, attended_sum, o_send, o_recv,
-    in_sem, table_sem, send_sem, recv_sem, back_send_sem, back_recv_sem,
+    in_sem, table_sem, taps_send_sem, taps_recv_sem, send_sem, recv_sem, back_send_sem, back_recv_sem,
     w_sem, sib_send_sem, sib_recv_sem, y_send_sem, y_recv_sem, near_send_sem, near_recv_sem,
     q_send_sem, q_recv_sem, o_send_sem, o_recv_sem,
     kz, k_own, k_left, k_right, k_far, k_sib, k_sent,
@@ -168,15 +186,20 @@
         [pl.ds(pl.multiple_of(h * 512 + base[g] * GROUP, 256), 256) for g in range(2)] for h in range(2)
     ]
     inputs = {}
+
+    def fetch(k, hbm, into, h, g):
+        inputs[k, h, g] = pltpu.make_async_copy(
+            hbm.at[:, cols_of[h][g]], into.at[h, g], in_sem.at[k, 2 * h + g]
+        )
+        inputs[k, h, g].start()
+
+    for g in range(2):
+        for h in range(2):
+            fetch(0, taps_hbm, taps_in, h, g)
     for h in range(2):
-        for k, (hbm, into) in enumerate(
-            ((taps_hbm, taps_in), (first_hbm, first_in), (value_hbm, value_in))
-        ):
-            for g in range(2):
-                inputs[k, h, g] = pltpu.make_async_copy(
-                    hbm.at[:, cols_of[h][g]], into.at[h, g], in_sem.at[k, 2 * h + g]
-                )
-                inputs[k, h, g].start()
+        for g in range(2):
+            fetch(1, first_hbm, first_in, h, g)
+            fetch(2, value_hbm, value_in, h, g)
 
     barrier = pltpu.get_barrier_semaphore()
 
@@ -201,11 +224,43 @@
 
     tables_in = []
     for k, (hbm, into) in enumerate((
-        (spread_hbm, spread_t), (turn_hbm, turn), (mix_hbm, mix_t), (unmix_hbm, unmix_t),
-        (gather_hbm, gather_t), (skip_hbm, skip),
+        (rows_hbm, rows_in), (cols_hbm, cols_in), (turn_hbm, turn), (skip_hbm, skip),
     )):
         tables_in.append(pltpu.make_async_copy(hbm, into, table_sem.at[k]))
         tables_in[-1].start()
+    def post_line(source, into, send_sems, recv_sems, g):
+        def one(k, carry):
+            o = lax.rem(me + k, 16)
+            pltpu.make_async_remote_copy(
+                src_ref=source.at[g, o], dst_ref=into.at[me], send_sem=send_sems, recv_sem=recv_sems,
+                device_id={"ctx": base[g] + o}, device_id_type=MESH,
+            ).start()
+            return carry
+
+        if g == 0:
+            pltpu.make_async_copy(source.at[0, lax.rem(me, 16)], into.at[me], recv_sems).start()
+        lax.fori_loop(1 if g == 0 else 0, 16, one, 0)
+
+    down = lax.broadcasted_iota(jnp.int32, (ROWS, ROWS), 0)
+    across = lax.broadcasted_iota(jnp.int32, (ROWS, ROWS), 1)
+    eye = jnp.where(down == across, 1.0, 0.0).astype(BF)
+    for g in range(2):
+        for h in range(2):
+            inputs[0, h, g].wait()
+            taps_send[g, :, h] = nt(eye, taps_in[h, g]).astype(BF).reshape(16, GROUP, ROWS)
+        if g == 0:
+            pl.semaphore_wait(barrier, CTX - 1 + 2 * ZS + 2)
+        post_line(taps_send, taps_recv, taps_send_sem.at[0], taps_recv_sem.at[0], g)
+    for h in range(2):
+        for g in range(2):
+            inputs[1, h, g].wait()
+            inputs[2, h, g].wait()
+            block = (first_in[h, g].astype(F32) * value_in[h, g].astype(F32)).astype(BF)
+            product[h, g] = block
+            send[h, g] = nt(eye, block).astype(BF).reshape(16, GROUP, ROWS)
+            post_line(send.at[h], recv.at[h], send_sem.at[h], recv_sem.at[h], g)
+    keys_of.scatter(keys_ref, 0, True)
+
     gates_in = []
     for h in range(2):
         for g in range(2):
@@ -213,42 +268,6 @@
                 second_hbm.at[:, cols_of[h][g]], second_in.at[h, g], in_sem.at[3, 2 * h + g]
             ))
             gates_in[-1].start()
-
-    def post_line(kind, h, g):
-        def one(k, carry):
-            o = lax.rem(me + k, 16)
-            pltpu.make_async_remote_copy(
-                src_ref=send.at[kind, h, g, o], dst_ref=recv.at[kind, h, me],
-                send_sem=send_sem.at[kind, h], recv_sem=recv_sem.at[kind, h],
-                device_id={"ctx": base[g] + o}, device_id_type=MESH,
-            ).start()
-            return carry
-
-        if g == 0:
-            pltpu.make_async_copy(
-                send.at[kind, h, 0, lax.rem(me, 16)], recv.at[kind, h, me], recv_sem.at[kind, h]
-            ).start()
-        lax.fori_loop(1 if g == 0 else 0, 16, one, 0)
-
-    down = lax.broadcasted_iota(jnp.int32, (ROWS, ROWS), 0)
-    across = lax.broadcasted_iota(jnp.int32, (ROWS, ROWS), 1)
-    eye = jnp.where(down == across, 1.0, 0.0).astype(BF)
-    for h in range(2):
-        for kind in (1, 0):
-            for g in range(2):
-                if kind == 1:
-                    inputs[0, h, g].wait()
-                    block = taps_in[h, g]
-                else:
-                    inputs[1, h, g].wait()
-                    inputs[2, h, g].wait()
-                    block = (first_in[h, g].astype(F32) * value_in[h, g].astype(F32)).astype(BF)
-                    product[h, g] = block
-                send[kind, h, g] = nt(eye, block).astype(BF).reshape(16, GROUP, ROWS)
-                if (h, kind, g) == (0, 1, 0):
-                    pl.semaphore_wait(barrier, CTX - 1 + 2 * ZS + 2)
-                post_line(kind, h, g)
-    keys_of.scatter(keys_ref, 0, True)
 
     order = [(other, lax.rem(y + k, YS)) for other in (1, 0) for k in (2, 1, 3, 0)]
     loads = []
@@ -260,16 +279,18 @@
         loads[-1].start()
     for copy in tables_in:
         copy.wait()
+    build_tables(rows_in, cols_in, eye, spread_t, mix_t, unmix_t, gather_t)
+    pltpu.make_async_copy(taps_recv, taps_recv, taps_recv_sem.at[0]).wait()
+    for h in range(2):
+        taps_spectrum[h] = spectrum(
+            taps_recv[:, h].reshape(half, ROWS), spread_t[...], mix_t[...], turn[:CTX], turn[CTX:]
+        )
 
     for h in range(2):
         tr, ti = turn[:CTX], turn[CTX:]
-        pltpu.make_async_copy(recv.at[1, h], recv.at[1, h], recv_sem.at[1, h]).wait()
-        taps_spectrum[...] = spectrum(
-            recv[1, h].reshape(half, ROWS), spread_t[...], mix_t[...], tr, ti
-        )
-        pltpu.make_async_copy(recv.at[0, h], recv.at[0, h], recv_sem.at[0, h]).wait()
-        d = spectrum(recv[0, h].reshape(half, ROWS), spread_t[...], mix_t[...], tr, ti)
-        e = taps_spectrum[...]
+        pltpu.make_async_copy(recv.at[h], recv.at[h], recv_sem.at[h]).wait()
+        d = spectrum(recv[h].reshape(half, ROWS), spread_t[...], mix_t[...], tr, ti)
+        e = taps_spectrum[h]
         d_re, d_im, e_re, e_im = d[:, :ROWS], d[:, ROWS:], e[:, :ROWS], e[:, ROWS:]
         y_re = (d_re * e_re - d_im * e_im).astype(BF)
         y_im = (d_re * e_im + d_im * e_re).astype(BF)
@@ -519,10 +540,11 @@
         attend_row(x2, i)
     pl.when(x == 2)(output_low)
 
+    some = taps_recv.at[pl.ds(0, CTX - 1)]
+    pltpu.make_async_copy(some, some, taps_send_sem.at[0]).wait()
     for h in range(2):
-        for kind in range(2):
-            some = recv.at[kind, h, pl.ds(0, CTX - 1)]
-            pltpu.make_async_copy(some, some, send_sem.at[kind, h]).wait()
+        some = recv.at[h, pl.ds(0, CTX - 1)]
+        pltpu.make_async_copy(some, some, send_sem.at[h]).wait()
         some = out_recv.at[h, pl.ds(0, CTX - 1)]
         pltpu.make_async_copy(some, some, back_send_sem.at[h]).wait()
     keys_of.scatter(keys_ref, 0, False)
@@ -566,8 +588,7 @@
 def per_device(
     first_input, second_input, value_input, filter_taps, skip_gain, out_weight, queries, keys
 ):
-    spread, mix, unmix, gather, turn_re, turn_im = tables()
-    consts = [jnp.asarray(t) for t in (spread, mix, unmix, gather, np.concatenate([turn_re, turn_im]))]
+    consts = [jnp.asarray(t) for t in tables()]
     dma = lambda *shape: pltpu.SemaphoreType.DMA(shape)
     bf = lambda *shape: pltpu.VMEM(shape, BF)
     fl = lambda *shape: pltpu.VMEM(shape, F32)
@@ -576,13 +597,15 @@
     mixed, attended = pl.pallas_call(
         whole_kernel,
         out_shape=(out, out),
-        in_specs=hbm(13),
+        in_specs=hbm(11),
         out_specs=tuple(vmem(2)),
         scratch_shapes=[
             bf(2, 2, ROWS, 256), bf(2, 2, ROWS, 256), bf(2, 2, ROWS, 256), bf(2, 2, ROWS, 256),
-            fl(1, 1024), bf(1024, 512), bf(512, 512), bf(512, 512), bf(512, 1024), fl(2 * CTX, ROWS),
+            fl(1, 1024), bf(2 * CTX, 512), bf(512, 256), fl(2 * CTX, ROWS),
+            bf(1024, 512), bf(512, 512), bf(512, 512), bf(512, 1024),
             bf(2, 2, ROWS, 256),
-            bf(2, 2, 2, 16, GROUP, ROWS), bf(2, 2, CTX, GROUP, ROWS), fl(512, 512),
+            bf(2, 2, 16, GROUP, ROWS), bf(2, CTX, GROUP, ROWS),
+            bf(2, 16, 2, GROUP, ROWS), bf(CTX, 2, GROUP, ROWS), fl(2, 512, 512),
             bf(2, CTX, GROUP, ROWS), bf(2, CTX, GROUP, ROWS),
             bf(ROWS, 1024),
             bf(8, 1024, HEAD), fl(8, ROWS, HEAD), fl(4, ROWS, HEAD), bf(4, ROWS, HEAD), bf(4, ROWS, HEAD),
@@ -590,7 +613,7 @@
             bf(XS, 2, ZS // 2, ROWS, HS), bf(XS, 2, ZS // 2, ROWS, HS), bf(4, ROWS, HS),
             fl(TOTAL // KEYS, KEYS // ROWS, ROWS, ROWS), bf(CHUNKS, ROWS, KEYS), fl(4, ROWS, 128), fl(4, ROWS, HS),
             bf(4, ROWS, HS), bf(4, ROWS, HS),
-            dma(4, 4), dma(6), dma(2, 2), dma(2, 2), dma(2), dma(2),
+            dma(4, 4), dma(4), dma(1), dma(1), dma(2), dma(2), dma(2), dma(2),
             dma(8), dma(4), dma(4), dma(2, PARTS), dma(2, PARTS), dma(2, PARTS), dma(2, PARTS),
             dma(4), dma(4), dma(4), dma(4),
         ] + sems(1) + sems(PARTS),

time: 103 us -> 103 us (level)
  no operation moved by 1% of the time
where the time goes in v7:
time: 103 us; the launch traced here: 102 us
  Pallas kernels  102 us (99%)
    pallas_call x1, Pallas kernels, per_device(): pl.pallas_call(whole_kernel, out_shape=(out, out), in_specs=hbm(11), out_...  99.9 us

profile of v7, /device:TPU:6, one launch (start us, length us, event | category | flops | bytes accessed | tf_op | source)
XLA Modules:
  0.0 102.4 jit_solution(1573723136979224777)
XLA Ops:
  0.6 99.9 %whole.1 = (bf16[256,512]{1,0:T(8,128)(2,1)}, bf16[256,512]{1,0:T(8,128)(2,1)}) custom-call(bf16[256,1024]{1,0:T(8,128)(2,1)} %first_hbm.1, bf16[256,1024]{1,0:T(8,128)(2,1)} %second_hbm.1, bf16[256,1024]{1,0:T(8,128)(2,1)} %value_hbm.1, bf16[256,1024]{1,0:T(8,128)(2,1)} %taps_hbm.1, f32[1,1024]{1,0:T(1,128)} %bitcast.1, bf16[1024,4096]{1,0:T(8,128)(2,1)} %weight_ref.1, ...), custom_call_target="tpu_custom_call" | custom-call | tf_op jit(solution)/shard_map/whole/pallas_call | solution.py:597
  100.6 1.8 %hand_over.1 = (bf16[256,512]{1,0:T(8,128)(2,1)}, bf16[256,512]{1,0:T(8,128)(2,1)}) custom-call(bf16[256,512]{1,0:T(8,128)(2,1)} %get-tuple-element.4.a, bf16[256,512]{1,0:T(8,128)(2,1)} %get-tuple-element.5.b), custom_call_target="tpu_custom_call" | custom-call | tf_op jit(solution)/shard_map/hand_over/pallas_call | solution.py:626

commit v8 on v7

--- a/solution.py
+++ b/solution.py
@@ -259,7 +259,6 @@
             product[h, g] = block
             send[h, g] = nt(eye, block).astype(BF).reshape(16, GROUP, ROWS)
             post_line(send.at[h], recv.at[h], send_sem.at[h], recv_sem.at[h], g)
-    keys_of.scatter(keys_ref, 0, True)
 
     gates_in = []
     for h in range(2):
@@ -289,6 +288,8 @@
     for h in range(2):
         tr, ti = turn[:CTX], turn[CTX:]
         pltpu.make_async_copy(recv.at[h], recv.at[h], recv_sem.at[h]).wait()
+        if h == 1:
+            keys_of.scatter(keys_ref, 0, True)
         d = spectrum(recv[h].reshape(half, ROWS), spread_t[...], mix_t[...], tr, ti)
         e = taps_spectrum[h]
         d_re, d_im, e_re, e_im = d[:, :ROWS], d[:, ROWS:], e[:, :ROWS], e[:, ROWS:]
@@ -313,10 +314,6 @@
 
         pltpu.make_async_copy(out_send.at[h, me], out_recv.at[h, me], back_recv_sem.at[h]).start()
         lax.fori_loop(1, CTX, reply, 0)
-        if h == 0:
-            keys_of.step_own(0)
-        else:
-            keys_of.step_near(0)
 
     for copy in gates_in:
         copy.wait()
@@ -336,6 +333,7 @@
     for k in range(8):
         loads[k].wait()
         partial[k] = nn(low, weights[k, :512])
+    keys_of.step_own(0)
     gate(1)
     high = gated_ref[:, 512:]
 
@@ -399,7 +397,7 @@
             far_hops[h, p].start()
     for k in range(1, 4):
         own_part[k] = chip_sum(k)
-    keys_of.step_far(0)
+    keys_of.step_near(0)
     for p in range(PARTS):
         for h in range(2):
             far_hops[h, p].wait_recv()
@@ -407,8 +405,7 @@
             near_send[h, spans[p]] = own_part[1 + h, spans[p]].astype(BF)
             near_hops[h, p] = hop(near_send, near_recv, near_send_sem, near_recv_sem, h, p)
             near_hops[h, p].start()
-    for row in range(XS):
-        keys_of.finish(row, 1)
+    keys_of.step_far(0)
 
     scale = 1.0 / math.sqrt(HS) * math.log2(math.e)
     blocks, first_step = [], []
@@ -476,14 +473,17 @@
         values_of.scatter(mine, p, True)
         mixed_ref[spans[p]] = mixed
 
-    for i in range(2):
-        score_all(i)
-        weigh_all(i)
     values_out(0)
+    for row in range(XS):
+        keys_of.finish(row, 1)
+    score_all(0)
+    weigh_all(0)
+    values_out(1)
+    score_all(1)
+    weigh_all(1)
     score_all(2)
-    values_out(1)
+    values_of.step_own(0)
     weigh_all(2)
-    values_of.step_own(0)
     score_all(3)
     values_of.step_own(1)
     weigh_half(3, 0)

time: 103 us -> 102 us (level)
  Pallas kernels: 102 us -> 99.9 us
    pallas_call x1, Pallas kernels: 99.9 us -> 98.1 us  [per_device(): pl.pallas_call(whole_kernel, out_shape=(out, out), in_specs=hbm(11), out_...]
where the time goes in v8:
time: 102 us; the launch traced here: 101 us
  Pallas kernels  99.9 us (98%)
    pallas_call x1, Pallas kernels, per_device(): pl.pallas_call(whole_kernel, out_shape=(out, out), in_specs=hbm(11), out_...  98.1 us

profile of v8, /device:TPU:6, one launch (start us, length us, event | category | flops | bytes accessed | tf_op | source)
XLA Modules:
  0.0 100.5 jit_solution(934271320678587638)
XLA Ops:
  0.6 98.1 %whole.1 = (bf16[256,512]{1,0:T(8,128)(2,1)}, bf16[256,512]{1,0:T(8,128)(2,1)}) custom-call(bf16[256,1024]{1,0:T(8,128)(2,1)} %first_hbm.1, bf16[256,1024]{1,0:T(8,128)(2,1)} %second_hbm.1, bf16[256,1024]{1,0:T(8,128)(2,1)} %value_hbm.1, bf16[256,1024]{1,0:T(8,128)(2,1)} %taps_hbm.1, f32[1,1024]{1,0:T(1,128)} %bitcast.1, bf16[1024,4096]{1,0:T(8,128)(2,1)} %weight_ref.1, ...), custom_call_target="tpu_custom_call" | custom-call | tf_op jit(solution)/shard_map/whole/pallas_call | solution.py:597
  98.7 1.8 %hand_over.1 = (bf16[256,512]{1,0:T(8,128)(2,1)}, bf16[256,512]{1,0:T(8,128)(2,1)}) custom-call(bf16[256,512]{1,0:T(8,128)(2,1)} %get-tuple-element.4.a, bf16[256,512]{1,0:T(8,128)(2,1)} %get-tuple-element.5.b), custom_call_target="tpu_custom_call" | custom-call | tf_op jit(solution)/shard_map/hand_over/pallas_call | solution.py:626

commit v9 on v8

--- a/solution.py
+++ b/solution.py
@@ -300,20 +300,27 @@
         b_im = b[:, ROWS:].reshape(GROUP, CTX, ROWS)
         c_re = (b_re * tr + b_im * ti).reshape(half, ROWS).astype(BF)
         c_im = (b_im * tr - b_re * ti).reshape(half, ROWS).astype(BF)
-        out = nn(gather_t[...], jnp.concatenate([c_re, c_im], axis=0))
-        out_send[h] = out.astype(BF).reshape(CTX, GROUP, ROWS)
-
-        def reply(k, carry, h=h):
-            to = lax.rem(me + k, CTX)
-            pltpu.make_async_remote_copy(
-                src_ref=out_send.at[h, to], dst_ref=out_recv.at[h, me],
-                send_sem=back_send_sem.at[h], recv_sem=back_recv_sem.at[h],
-                device_id={"ctx": to}, device_id_type=MESH,
-            ).start()
-            return carry
-
-        pltpu.make_async_copy(out_send.at[h, me], out_recv.at[h, me], back_recv_sem.at[h]).start()
-        lax.fori_loop(1, CTX, reply, 0)
+        points = jnp.concatenate([c_re, c_im], axis=0)
+        for g in range(2):
+            rows = pl.ds(pl.multiple_of(base[g] * GROUP, 256), 256)
+            out_send[h, pl.ds(base[g], 16)] = (
+                nn(gather_t[rows], points).astype(BF).reshape(16, GROUP, ROWS)
+            )
+
+            def reply(k, carry, h=h, g=g):
+                to = base[g] + lax.rem(me + k, 16)
+                pltpu.make_async_remote_copy(
+                    src_ref=out_send.at[h, to], dst_ref=out_recv.at[h, me],
+                    send_sem=back_send_sem.at[h], recv_sem=back_recv_sem.at[h],
+                    device_id={"ctx": to}, device_id_type=MESH,
+                ).start()
+                return carry
+
+            if g == 0:
+                pltpu.make_async_copy(
+                    out_send.at[h, me], out_recv.at[h, me], back_recv_sem.at[h]
+                ).start()
+            lax.fori_loop(1 if g == 0 else 0, 16, reply, 0)
 
     for copy in gates_in:
         copy.wait()
@@ -362,7 +369,8 @@
         start_either(*query_copies(j))
 
     swaps = []
-    for k in range(4):
+
+    def swap(k):
         sib_send[k] = projected(k).astype(BF)
         swaps.append(pltpu.make_async_remote_copy(
             src_ref=sib_send.at[k], dst_ref=sib_recv.at[k],
@@ -370,6 +378,8 @@
             device_id={"tp": y * 2 + 1 - c}, device_id_type=MESH,
         ))
         swaps[-1].start()
+
+    swap(0)
 
     def chip_sum(k):
         own = projected(4 + k)
@@ -395,6 +405,8 @@
         for h in range(2):
             far_hops[h, p] = hop(y_send, y_recv, y_send_sem, y_recv_sem, h, p)
             far_hops[h, p].start()
+    for k in range(1, 4):
+        swap(k)
     for k in range(1, 4):
         own_part[k] = chip_sum(k)
     keys_of.step_near(0)

time: 102 us -> 101 us (level)
  no operation moved by 1% of the time
where the time goes in v9:
time: 101 us; the launch traced here: 100 us
  Pallas kernels  99.4 us (98%)
    pallas_call x1, Pallas kernels, per_device(): pl.pallas_call(whole_kernel, out_shape=(out, out), in_specs=hbm(11), out_...  97.5 us

profile of v9, /device:TPU:6, one launch (start us, length us, event | category | flops | bytes accessed | tf_op | source)
XLA Modules:
  0.0 100.0 jit_solution(4015530633035345674)
XLA Ops:
  0.6 97.5 %whole.1 = (bf16[256,512]{1,0:T(8,128)(2,1)}, bf16[256,512]{1,0:T(8,128)(2,1)}) custom-call(bf16[256,1024]{1,0:T(8,128)(2,1)} %first_hbm.1, bf16[256,1024]{1,0:T(8,128)(2,1)} %second_hbm.1, bf16[256,1024]{1,0:T(8,128)(2,1)} %value_hbm.1, bf16[256,1024]{1,0:T(8,128)(2,1)} %taps_hbm.1, f32[1,1024]{1,0:T(1,128)} %bitcast.1, bf16[1024,4096]{1,0:T(8,128)(2,1)} %weight_ref.1, ...), custom_call_target="tpu_custom_call" | custom-call | tf_op jit(solution)/shard_map/whole/pallas_call | solution.py:609
  98.2 1.8 %hand_over.1 = (bf16[256,512]{1,0:T(8,128)(2,1)}, bf16[256,512]{1,0:T(8,128)(2,1)}) custom-call(bf16[256,512]{1,0:T(8,128)(2,1)} %get-tuple-element.4.a, bf16[256,512]{1,0:T(8,128)(2,1)} %get-tuple-element.5.b), custom_call_target="tpu_custom_call" | custom-call | tf_op jit(solution)/shard_map/hand_over/pallas_call | solution.py:638

commit v10 on v9

--- a/solution.py
+++ b/solution.py
@@ -493,15 +493,14 @@
     values_out(1)
     score_all(1)
     weigh_all(1)
+    values_of.step_own(0)
     score_all(2)
-    values_of.step_own(0)
+    values_of.step_own(1)
     weigh_all(2)
+    values_of.step_near(0)
     score_all(3)
-    values_of.step_own(1)
-    weigh_half(3, 0)
-    values_of.step_near(0)
-    weigh_half(3, 1)
     values_of.step_near(1)
+    weigh_all(3)
 
     def output_copies(i):
         row, zq, rank, last = blocks[i]

time: 101 us -> 99.8 us (0.988)
  no operation moved by 1% of the time
where the time goes in v10:
time: 99.8 us; the launch traced here: 99.1 us
  Pallas kernels  98.4 us (99%)
    pallas_call x1, Pallas kernels, per_device(): pl.pallas_call(whole_kernel, out_shape=(out, out), in_specs=hbm(11), out_...  96.6 us

profile of v10, /device:TPU:6, one launch (start us, length us, event | category | flops | bytes accessed | tf_op | source)
XLA Modules:
  0.0 99.1 jit_solution(10265382434073748843)
XLA Ops:
  0.6 96.6 %whole.1 = (bf16[256,512]{1,0:T(8,128)(2,1)}, bf16[256,512]{1,0:T(8,128)(2,1)}) custom-call(bf16[256,1024]{1,0:T(8,128)(2,1)} %first_hbm.1, bf16[256,1024]{1,0:T(8,128)(2,1)} %second_hbm.1, bf16[256,1024]{1,0:T(8,128)(2,1)} %value_hbm.1, bf16[256,1024]{1,0:T(8,128)(2,1)} %taps_hbm.1, f32[1,1024]{1,0:T(1,128)} %bitcast.1, bf16[1024,4096]{1,0:T(8,128)(2,1)} %weight_ref.1, ...), custom_call_target="tpu_custom_call" | custom-call | tf_op jit(solution)/shard_map/whole/pallas_call | solution.py:608
  97.2 1.8 %hand_over.1 = (bf16[256,512]{1,0:T(8,128)(2,1)}, bf16[256,512]{1,0:T(8,128)(2,1)}) custom-call(bf16[256,512]{1,0:T(8,128)(2,1)} %get-tuple-element.4.a, bf16[256,512]{1,0:T(8,128)(2,1)} %get-tuple-element.5.b), custom_call_target="tpu_custom_call" | custom-call | tf_op jit(solution)/shard_map/hand_over/pallas_call | solution.py:637
